TPU v7x, 128 devices: a whole 4x4x4 slice. The times are simulated.
128 devices in a mesh: fsdp: 8 (over x, z_lo), sp: 16 (over z_hi, y, core).
Axes of the slice: x: 4, y: 4, z: 4 (z_hi: 2, z_lo: 2; z = z_hi * 2 + z_lo), core: 2. Of those that a mesh axis runs over, the one named last changes fastest.
Arguments:
- queries: bfloat16 [8, 2, 2048, 2048], P('fsdp', None, 'sp'), may hold values from -130 to 130
- span_keys: bfloat16 [8, 2, 2048, 512], P('fsdp', None, 'sp'), may hold values from -10 to 10
- span_values: bfloat16 [8, 2, 2048, 512], P('fsdp', None, 'sp'), may hold values from -18 to 18
- cotangent: bfloat16 [8, 2, 2048, 2048], P('fsdp', None, 'sp'), may hold values from -6 to 6
- cache_keys: bfloat16 [1024, 512], P('fsdp', 'sp'), may hold values from -9 to 9
- cache_values: bfloat16 [1024, 512], P('fsdp', 'sp'), may hold values from -18 to 18
- hist_count: int32 [8], replicated, may hold values from 1 to 2
- span_ids: int32 [8, 2], replicated, may hold values from 9 to 16
Outputs:
- attended_out: bfloat16 [8, 2, 2048, 2048], P('fsdp', None, 'sp')
- grad_queries: bfloat16 [8, 2, 2048, 2048], P('fsdp', None, 'sp')
- grad_keys: bfloat16 [8, 2, 2048, 512], P('fsdp', None, 'sp')
- grad_values: bfloat16 [8, 2, 2048, 512], P('fsdp', None, 'sp')
- grad_cache_keys: float32 [1024, 512], P('fsdp', 'sp')
- grad_cache_values: float32 [1024, 512], P('fsdp', 'sp')
All inputs are finite; a program needn't handle non-finite values.
Results may differ from a plain program's by a relative error of at most 0.019.
Values may be sent and summed in bfloat16 or wider, within the bound.
No kernel may reach another device: no remote copies, remote signals or barrier semaphores. Data moves between devices by JAX's collectives and lax.ppermute only.
A program may use at most 128 MiB of HBM per device.

v0:
```python
import functools
import math

import jax
import jax.numpy as jnp
from jax import lax
from jax.experimental import pallas as pl
from jax.experimental.pallas import tpu as pltpu
from jax.sharding import Mesh
from jax.sharding import PartitionSpec as P

BF = jnp.bfloat16
F32 = jnp.float32
HEADS = 4
KVH = 4
D = 128
TB = 128
ROWS = HEADS * TB
CK = 256
HIST = 1024
SPAN = 2048
NROW = HIST + SPAN
NCH = NROW // CK
SCALE = 1.0 / math.sqrt(D)
C2 = SCALE * math.log2(math.e)
NEG = -1e30
STEP1, STEP2, STEP3 = 5, 5, 5
SP = ("zhi", "y", "core")
FS = ("x", "zlo")


def dg(a, b, ca, cb):
    return lax.dot_general(a, b, (((ca,), (cb,)), ((), ())), preferred_element_type=F32)


def pieces(x):
    a = x.astype(BF)
    r = x - a.astype(F32)
    b = r.astype(BF)
    c = (r - b.astype(F32)).astype(BF)
    return a, b, c


def at_cols(x, rows):
    ln = lax.broadcasted_iota(jnp.int32, (rows, D), 1)
    out = jnp.zeros((rows, D), F32)
    for k, p in enumerate(pieces(x)):
        out = jnp.where(ln == k, p.astype(F32), out)
    return out


def span_kernel(
    ordinal, pos_ref, cnt_ref, ids_ref, *rest
):
    last = ordinal == 1
    qg_hbm, rest = (rest[:4], rest[4:]) if last else (rest[:1], rest[1:])
    gathered, rest = rest[:4], rest[4:]
    if last:
        acc_ref, *rest = rest
    first_kv = ordinal * (4 * TB + 8 * 32)
    *out_refs, keep_ref, send_ref, hg_ref = rest[:7]
    rest = rest[7:]
    (ks, vs, q_s, ga_s, qt_s, gt_s, s_s, w_s, mx, o_s, dq_s, dkt, dvt, qg_ref, o_b, h_s, sem) = rest
    zhi, y_me, core, x_me, zlo = pos_ref[0], pos_ref[1], pos_ref[2], pos_ref[3], pos_ref[4]
    f_me = x_me * 2 + zlo
    if last:
        fetches = [
            pltpu.make_async_copy(qg_hbm[sh], qg_ref.at[lax.rem(y_me - sh + 4, 4)], sem.at[sh]) for sh in range(4)
        ]
    else:
        fetches = [pltpu.make_async_copy(qg_hbm[0], qg_ref, sem.at[0])]
    for fetch in fetches:
        fetch.start()
    span_id = ids_ref[f_me, ordinal]
    see = [(cnt_ref[f] > 1) & (f + 8 < span_id) for f in range(8)]
    vs[:, D:] = jnp.ones((NROW, D), BF)
    n1 = jnp.int32(0)
    for f in range(8):
        n1 = n1 + see[f].astype(jnp.int32)
    nh1 = (n1 + 3) // 4
    ln = lax.broadcasted_iota(jnp.int32, (HIST, D), 1)
    rw = lax.broadcasted_iota(jnp.int32, (HIST, D), 0)
    ks[0:HIST, D:] = jnp.where((ln == 0) & (rw >= 512 + n1 * 64), NEG, 0.0).astype(BF)
    base = pl.multiple_of(512 + nh1 * CK, CK)
    n = jnp.int32(0)

    for rel in range(4):
        for i in range(8):
            h_s[rel, i] = gathered[rel][4 * TB + i * 32 : 4 * TB + (i + 1) * 32, :]

    def history(f, piece):
        rel = (zhi ^ (piece // 2)) * 2 + (core ^ (piece % 2))
        return h_s[rel, (zlo ^ (f % 2)) * 4 + lax.rem(x_me - f // 2 + 4, 4)]

    for f in range(8):
        cols = jnp.concatenate([history(f, p) for p in range(4)], axis=0)
        rows = jnp.concatenate([cols[:, 0:TB].T, cols[:, TB:].T], axis=1)
        ks[f * 64 : (f + 1) * 64, 0:D] = rows[0:64, 0:D]
        vs[f * 64 : (f + 1) * 64, 0:D] = rows[0:64, D:]
        at = pl.multiple_of(512 + n * 64, 64)
        ks[pl.ds(at, 64), 0:D] = rows[64:, 0:D]
        vs[pl.ds(at, 64), 0:D] = rows[64:, D:]
        n = n + see[f].astype(jnp.int32)
    for r in range(4):

        @pl.when(n1 + r < nh1 * 4)
        def _(r=r):
            at = pl.multiple_of(512 + (n1 + r) * 64, 64)
            ks[pl.ds(at, 64), 0:D] = jnp.zeros((64, D), BF)
            vs[pl.ds(at, 64), 0:D] = jnp.zeros((64, D), BF)

    for rel in range(4):
        z = zhi if rel < 2 else 1 - zhi
        c = core if rel % 2 == 0 else 1 - core
        for sh in range(4):
            yy = lax.rem(y_me - sh + 4, 4)
            at = pl.multiple_of(base + z * 1024 + yy * 256 + c * 128, 128)
            part = gathered[rel][first_kv + sh * TB : first_kv + (sh + 1) * TB, :]
            ks[pl.ds(at, 128), 0:D] = part[:, 0:D]
            ks[pl.ds(at, 128), D:] = jnp.zeros((128, D), BF)
            vs[pl.ds(at, 128), 0:D] = part[:, D:]
    dkt[...] = jnp.zeros_like(dkt)
    dvt[...] = jnp.zeros_like(dvt)
    lnr = lax.broadcasted_iota(jnp.int32, (ROWS, D), 1)
    lane = lax.broadcasted_iota(jnp.int32, (ROWS, CK), 1)
    tok = lax.broadcasted_iota(jnp.int32, (ROWS, CK), 0) % TB + core * TB
    q_s[:, D:] = jnp.where(lnr == 0, 1.0, 0.0).astype(BF)

    def chunk(i, n):
        return pl.ds(pl.multiple_of(i * CK, CK), n * CK)

    def block(b, carry):
        for h in range(HEADS):
            q_s[h * TB : (h + 1) * TB, 0:D] = qg_ref[b, :, h * D : (h + 1) * D]
            ga_s[h * TB : (h + 1) * TB, 0:D] = qg_ref[b, :, (HEADS + h) * D : (HEADS + h + 1) * D]
        mx[...] = jnp.full_like(mx, NEG)
        nfull = 2 + nh1 + zhi * 4 + b

        def walk(fn, step):
            groups = nfull // step

            def one(i, carry):
                fn(step * i, step, False)
                return carry

            lax.fori_loop(0, groups, one, 0)
            for r in range(step):

                @pl.when(nfull - groups * step == r)
                def _(r=r):
                    fn(nfull - r, r + 1, True)

        def scores(i, n, diag):
            s = dg(q_s[...], ks[chunk(i, n), :], 1, 1)
            parts = [s[:, k * CK : (k + 1) * CK] for k in range(n)]
            if diag:
                parts[-1] = jnp.where(lane <= tok, parts[-1], NEG)
            for k in range(n):
                s_s[i + k] = parts[k]
            cols = [p[:, h * D : (h + 1) * D] for p in parts for h in range(2)]
            mx[...] = functools.reduce(jnp.maximum, cols, mx[...])

        walk(scores, STEP1)
        m = jnp.max(mx[...], axis=1, keepdims=True)
        mx[...] = jnp.broadcast_to(m * C2, (ROWS, D))
        o_s[...] = jnp.zeros_like(o_s)

        def weigh(i, n, diag):
            mm = mx[...]
            mm = jnp.concatenate([mm, mm], axis=1)
            ws = [jnp.exp2(s_s[i + k] * C2 - mm).astype(BF) for k in range(n)]
            for k in range(n):
                w_s[i + k] = ws[k]
            o_s[...] += dg(jnp.concatenate(ws, axis=1), vs[chunk(i, n), :], 1, 0)

        walk(weigh, STEP2)
        inv = 1.0 / o_s[:, D:]
        att = (o_s[:, :D] * inv).astype(BF)
        gp = (ga_s[:, 0:D].astype(F32) * inv).astype(BF)
        ga_s[:, 0:D] = gp
        for h in range(HEADS):
            o_b[:, h * D : (h + 1) * D] = att[h * TB : (h + 1) * TB, :]
        delta = jnp.sum(gp.astype(F32) * att.astype(F32), axis=1, keepdims=True)
        ga_s[:, D:] = at_cols(-delta, ROWS).astype(BF)
        qt_s[...] = q_s[:, 0:D].T
        gt_s[...] = gp.T
        dq_s[...] = jnp.zeros_like(dq_s)

        def back(i, n, diag):
            dp = dg(ga_s[...], vs[chunk(i, n), :], 1, 1).astype(BF)
            ws = [w_s[i + k] for k in range(n)]
            dss = [ws[k] * dp[:, k * CK : (k + 1) * CK] for k in range(n)]
            dq_s[...] += dg(jnp.concatenate(dss, axis=1), ks[chunk(i, n), 0:D], 1, 0)
            for k in range(n):
                dkt[i + k] += dg(qt_s[...], dss[k], 1, 0)
                dvt[i + k] += dg(gt_s[...], ws[k], 1, 0)

        walk(back, STEP3)
        dqv = (dq_s[...] * SCALE).astype(BF)
        for h in range(HEADS):
            o_b[:, (HEADS + h) * D : (HEADS + h + 1) * D] = dqv[h * TB : (h + 1) * TB, :]
        for sh in range(4):

            @pl.when(lax.rem(y_me - b + 4, 4) == sh)
            def _(sh=sh):
                out_refs[sh][...] = o_b[...]

        return carry

    for fetch in fetches:
        fetch.wait()
    lax.fori_loop(0, 4, block, 0)

    for rel in range(4):
        z = zhi if rel < 2 else 1 - zhi
        c = core if rel % 2 == 0 else 1 - core
        for sh in range(4):
            yy = lax.rem(y_me - sh + 4, 4)
            i = 2 + nh1 + z * 4 + yy
            half = pl.ds(pl.multiple_of(c * 128, 128), 128)
            if last:
                ref, at = (keep_ref, send_ref)[rel % 2], rel // 2
            else:
                ref, at = (keep_ref, send_ref)[rel // 2], rel % 2
            ref[at, sh, :, 0:D] = (dkt[i, :, half] * SCALE).T.astype(BF)
            ref[at, sh, :, D:] = dvt[i, :, half].T.astype(BF)
    for i in range(4):

        @pl.when(i < 2 + nh1)
        def _(i=i):
            s_s[0, 0:CK, 0:D] = (dkt[i] * SCALE).T
            s_s[0, 0:CK, D:] = dvt[i].T
            s_s[1 + i // 2, (i % 2) * CK : (i % 2 + 1) * CK, :] = s_s[0, 0:CK, :]

    n = jnp.int32(0)
    for f in range(8):
        first = s_s[1, f * 64 : (f + 1) * 64, :]
        second = s_s[2, pl.ds(pl.multiple_of(n * 64, 64), 64), :]
        second = jnp.where(see[f], second, 0.0)
        n = n + see[f].astype(jnp.int32)
        if last:
            first = first + acc_ref[f, 0:64, :]
            second = second + acc_ref[f, 64:128, :]
            both = jnp.concatenate([first, second], axis=0).T.astype(BF)
            for p in range(4):
                hg_ref[f, p, 0] = both[p * 32 : (p + 1) * 32]
                hg_ref[f, p, 1] = both[D + p * 32 : D + (p + 1) * 32]
        else:
            hg_ref[f, 0:64, :] = first
            hg_ref[f, 64:128, :] = second


def span_call(ordinal, pos, cnt, ids, qg, gathered, acc=None):
    last = ordinal == 1
    smem = pl.BlockSpec(memory_space=pltpu.SMEM)
    vmem = pl.BlockSpec(memory_space=pltpu.VMEM)
    extra = (acc,) if last else ()
    out = (jax.ShapeDtypeStruct((TB, 2 * HEADS * D), BF),) * 4
    hg = jax.ShapeDtypeStruct((8, 4, 2, 32, TB), BF) if last else jax.ShapeDtypeStruct((8, TB, 2 * D), F32)
    return pl.pallas_call(
        functools.partial(span_kernel, ordinal),
        out_shape=out
        + (jax.ShapeDtypeStruct((2, 4, TB, 2 * D), BF),) * 2
        + (hg,),
        in_specs=[smem] * 3 + [pl.BlockSpec(memory_space=pl.ANY)] * len(qg) + [vmem] * (4 + len(extra)),
        out_specs=(vmem,) * (len(out) + 3),
        scratch_shapes=[
            pltpu.VMEM((NROW, 2 * D), BF),
            pltpu.VMEM((NROW, 2 * D), BF),
            pltpu.VMEM((ROWS, 2 * D), BF),
            pltpu.VMEM((ROWS, 2 * D), BF),
            pltpu.VMEM((D, ROWS), BF),
            pltpu.VMEM((D, ROWS), BF),
            pltpu.VMEM((NCH, ROWS, CK), F32),
            pltpu.VMEM((NCH, ROWS, CK), BF),
            pltpu.VMEM((ROWS, D), F32),
            pltpu.VMEM((ROWS, 2 * D), F32),
            pltpu.VMEM((ROWS, D), F32),
            pltpu.VMEM((NCH, D, CK), F32),
            pltpu.VMEM((NCH, D, CK), F32),
            pltpu.VMEM((4, TB, 2 * HEADS * D), BF),
            pltpu.VMEM((TB, 2 * HEADS * D), BF),
            pltpu.VMEM((4, 8, 32, 2 * D), BF),
            pltpu.SemaphoreType.DMA((4,)),
        ],
        compiler_params=pltpu.CompilerParams(vmem_limit_bytes=40 * 2**20),
        cost_estimate=pl.CostEstimate(flops=int(2.5e10), bytes_accessed=6 * 2**20, transcendentals=0),
    )(pos, cnt, ids, *qg, *gathered, *extra)


def split_shifts_kernel(pos_ref, a_ref, b_ref, *outs):
    for sh in range(4):
        at = pl.ds(pl.multiple_of(lax.rem(pos_ref[1] + sh, 4) * D, D), D)
        for j in range(2):
            outs[sh][j, :, 0:D] = a_ref[0, j, :, at]
            outs[sh][j, :, D:] = b_ref[0, j, :, at]


def join_shifts_kernel(pos_ref, p0, p1, p2, p3, a_ref, b_ref):
    for sh, part in enumerate((p0, p1, p2, p3)):
        at = pl.ds(pl.multiple_of(lax.rem(pos_ref[1] + sh, 4) * D, D), D)
        for j in range(2):
            a_ref[0, j, :, at] = part[j, :, 0:D]
            b_ref[0, j, :, at] = part[j, :, D:]


def copy_all(pairs, sem):
    copies = [pltpu.make_async_copy(src, dst, sem.at[i]) for i, (src, dst) in enumerate(pairs)]
    for c in copies:
        c.start()
    for c in copies:
        c.wait()


def split_heads_kernel(pos_ref, a_ref, b_ref, out0, s0, s1, s2, s3, sem):
    width = HEADS * D
    pairs = []
    for y in range(4):
        at = pl.ds(y * width, width)
        pairs.append((a_ref.at[0, 0, :, at], out0.at[y, :, pl.ds(0, width)]))
        pairs.append((b_ref.at[0, 0, :, at], out0.at[y, :, pl.ds(width, width)]))
    for sh, part in enumerate((s0, s1, s2, s3)):
        at = pl.ds(pl.multiple_of(lax.rem(pos_ref[1] + sh, 4) * width, D), width)
        pairs.append((a_ref.at[0, 1, :, at], part.at[:, pl.ds(0, width)]))
        pairs.append((b_ref.at[0, 1, :, at], part.at[:, pl.ds(width, width)]))
    copy_all(pairs, sem)


def join_heads_kernel(pos_ref, *refs):
    width = HEADS * D
    a_ref, b_ref, sem = refs[8:]
    pairs = []
    for sh in range(4):
        at = pl.ds(pl.multiple_of(lax.rem(pos_ref[1] + sh, 4) * width, D), width)
        for j in range(2):
            pairs.append((refs[4 * j + sh].at[:, pl.ds(0, width)], a_ref.at[0, j, :, at]))
            pairs.append((refs[4 * j + sh].at[:, pl.ds(width, width)], b_ref.at[0, j, :, at]))
    copy_all(pairs, sem)


def relayout(kernel, outs, args, with_pos, copies=0):
    ref = pl.BlockSpec(memory_space=pl.ANY if copies else pltpu.VMEM)
    specs = [ref] * len(args)
    if with_pos:
        specs[0] = pl.BlockSpec(memory_space=pltpu.SMEM)
    size = 2 * sum(a.size * 2 for a in args)
    return pl.pallas_call(
        kernel,
        out_shape=tuple(jax.ShapeDtypeStruct(o, BF) for o in outs),
        in_specs=specs,
        out_specs=(ref,) * len(outs),
        scratch_shapes=[pltpu.SemaphoreType.DMA((copies,))] if copies else [],
        cost_estimate=pl.CostEstimate(flops=0, bytes_accessed=size, transcendentals=0),
        compiler_params=pltpu.CompilerParams(vmem_limit_bytes=16 * 2**20),
    )(*args)


def y_exchange(a):
    return lax.all_to_all(a, "y", split_axis=0, concat_axis=0, tiled=True)


def y_shift(a, sh):
    return lax.ppermute(a, "y", [(i, (i + sh) % 4) for i in range(4)])


def flip(a, axis):
    return lax.ppermute(a, axis, [(0, 1), (1, 0)])


def linear(z, y, c):
    return z * 8 + y * 2 + c


def per_device(queries, span_keys, span_values, cotangent, cache_keys, cache_values, hist_count, span_ids):
    zhi, y_me, core = lax.axis_index("zhi"), lax.axis_index("y"), lax.axis_index("core")
    pos = jnp.stack([zhi, y_me, core, lax.axis_index("x"), lax.axis_index("zlo")]).astype(jnp.int32)

    cache = jnp.concatenate([cache_keys.T, cache_values.T], axis=1)
    perm = []
    for head in range(KVH):
        for p in range(4):
            perm.append((linear(head // 2, 2 * (head % 2) + p // 2, p % 2), linear(p // 2, head, p % 2)))
    cache = lax.ppermute(cache, SP, perm)
    cache = jnp.stack([cache] + [lax.ppermute(cache, "x", [(i, (i + s) % 4) for i in range(4)]) for s in (1, 2, 3)])
    cache_x = cache
    cache = jnp.stack([cache, flip(cache, "zlo")]).reshape(8 * 32, 2 * D)
    kv_sent = relayout(split_shifts_kernel, [(2, TB, 2 * D)] * 4, (pos, span_keys, span_values), True)
    queries, kv_sent = lax.optimization_barrier((queries, kv_sent))
    wide = (TB, 2 * HEADS * D)
    sent0, *sent1 = relayout(
        split_heads_kernel, [(4,) + wide] + [wide] * 4, (pos, queries, cotangent), True, 16
    )
    kv_here = [kv_sent[0]] + [y_shift(kv_sent[sh], sh) for sh in (1, 2, 3)]
    own = jnp.concatenate([a[0] for a in kv_here] + [cache] + [a[1] for a in kv_here], axis=0)
    sent0, own = lax.optimization_barrier((sent0, own))
    qg0 = y_exchange(sent0)
    other = flip(own, "zhi")
    gathered = (own, flip(own, "core"), other, flip(other, "core"))
    sent1, _ = lax.optimization_barrier((sent1, other))
    qg1 = [sent1[0]] + [y_shift(sent1[sh], sh) for sh in (1, 2, 3)]
    out0 = span_call(0, pos, hist_count, span_ids, (qg0,), gathered)
    *out0, keep0, send0, acc = out0
    *out1, keep1, send1, hg = span_call(1, pos, hist_count, span_ids, qg1, gathered, acc)

    back0 = [out0[0]] + [y_shift(out0[sh], 4 - sh) for sh in (1, 2, 3)]
    got0 = flip(send0, "zhi")
    (out1, send1, hg, back0, got0) = lax.optimization_barrier((out1, send1, hg, back0, got0))
    sum0 = (keep0.astype(F32) + got0.astype(F32)).astype(BF)
    got1 = flip(send1, "core")
    back1 = [out1[0]] + [y_shift(out1[sh], 4 - sh) for sh in (1, 2, 3)]
    sum1 = (keep1.astype(F32) + got1.astype(F32)).astype(BF)
    hg, sum1 = lax.optimization_barrier((hg, sum1))
    hg = lax.all_to_all(hg.reshape(32, 2, 32, TB), FS + ("zhi", "core"), split_axis=0, concat_axis=0, tiled=True)
    got0 = flip(sum0[1], "core")
    got1 = flip(sum1[1], "zhi")
    red0 = sum0[0].astype(F32) + got0.astype(F32)
    red1 = sum1[0].astype(F32) + got1.astype(F32)
    red = jnp.stack([red0, red1], axis=1).astype(BF)
    back1, red = lax.optimization_barrier((back1, red))
    kv_back = [red[0]] + [y_shift(red[sh], 4 - sh) for sh in (1, 2, 3)]

    hgrad = lax.ppermute(jnp.sum(hg.astype(F32), axis=0), SP, [(b, a) for a, b in perm])
    attended, grad_q = relayout(join_heads_kernel, [(1, 2, TB, 4 * HEADS * D)] * 2, (pos, *back0, *back1), True, 16)
    grad_k, grad_v = relayout(join_shifts_kernel, [(1, 2, TB, 4 * D)] * 2, (pos, *kv_back), True)
    return attended, grad_q, grad_k, grad_v, hgrad[0].T, hgrad[1].T


def solution(mesh):
    fine = Mesh(mesh.devices.reshape(4, 2, 2, 4, 2), ("x", "zlo", "zhi", "y", "core"))
    tokens = P(FS, None, SP, None)
    resident = P(FS, SP)
    return jax.shard_map(
        per_device,
        mesh=fine,
        in_specs=(tokens,) * 4 + (resident,) * 2 + (P(), P()),
        out_specs=(tokens,) * 4 + (resident,) * 2,
        check_vma=False,
    )
```

profile of v0, /device:TPU:10, one launch (start us, length us, event | category | flops | bytes accessed | tf_op | source)
XLA Modules:
  0.0 140.1 jit_solution(13888736342069271828)
XLA Ops:
  0.6 0.7 pad_maximum_fusion.3
  1.4 5.7 %collective-permute-start.3 = (bf16[32,256]{1,0:T(8,128)(2,1)S(1)}, bf16[32,256]{1,0:T(8,128)(2,1)S(1)}, u32[]{:S(2)}, u32[]{:S(2)}) collective-permute-start(bf16[32,256]{1,0:T(8,128)(2,1)S(1)} %pad_maximum_fusion.3), channel_id=1, source_target_pairs={{0,0},{1,1},{2,8},{3,9},{4,2},{5,3},{6,10},{7,11},{8,4},{9,5},{10,... | collective-permute-start | bytes 49160 | tf_op jit(solution)/shard_map/ppermute | solution.py:383
  7.0 1.4 %collective-permute-done.3 = bf16[32,256]{1,0:T(8,128)(2,1)S(1)} collective-permute-done((bf16[32,256]{1,0:T(8,128)(2,1)S(1)}, bf16[32,256]{1,0:T(8,128)(2,1)S(1)}, u32[]{:S(2)}, u32[]{:S(2)}) %collective-permute-start.3) | collective-permute-done | bytes 16416 | tf_op jit(solution)/shard_map/ppermute | solution.py:383
  8.4 0.5 collective-permute-start.6
  9.0 2.4 %collective-permute-start.5 = (bf16[32,256]{1,0:T(8,128)(2,1)S(1)}, bf16[32,256]{1,0:T(8,128)(2,1)S(1)}, u32[]{:S(2)}, u32[]{:S(2)}) collective-permute-start(bf16[32,256]{1,0:T(8,128)(2,1)S(1)} %collective-permute-done.3), channel_id=1, source_target_pairs={{0,64},{32,96},{64,0},{96,32},{1,65},{33,97},{65,1},{97,33},{2,66}... | collective-permute-start | bytes 49160 | tf_op jit(solution)/shard_map/ppermute | solution.py:384
  11.4 1.8 %collective-permute-start.4 = (bf16[32,256]{1,0:T(8,128)(2,1)S(1)}, bf16[32,256]{1,0:T(8,128)(2,1)S(1)}, u32[]{:S(2)}, u32[]{:S(2)}) collective-permute-start(bf16[32,256]{1,0:T(8,128)(2,1)S(1)} %collective-permute-done.3), channel_id=1, source_target_pairs={{0,32},{32,64},{64,96},{96,0},{1,33},{33,65},{65,97},{97,1},{2,34}... | collective-permute-start | bytes 49160 | tf_op jit(solution)/shard_map/ppermute | solution.py:384
  13.2 0.1 stack.59.pos_ref
  13.3 0.9 copy-done.2
  14.2 0.9 copy-done.3
  15.2 0.6 shard_map.127
  15.8 4.1 %collective-permute-start = (bf16[2,128,256]{2,1,0:T(8,128)(2,1)S(1)}, bf16[2,128,256]{2,1,0:T(8,128)(2,1)S(1)}, u32[]{:S(2)}, u32[]{:S(2)}) collective-permute-start(bf16[2,128,256]{2,1,0:T(8,128)(2,1)S(1)} %get-tuple-element.73), channel_id=1, source_target_pairs={{0,2},{2,4},{4,6},{6,0},{1,3},{3,5},{5,7},{7,1},{8,10},{10,12},{12... | collective-permute-start | bytes 393224 | tf_op jit(solution)/shard_map/ppermute | solution.py:363
  19.9 0.0 collective-permute-start.1
  19.9 0.0 collective-permute-done.6
  19.9 2.2 %collective-permute-start.2 = (bf16[2,128,256]{2,1,0:T(8,128)(2,1)S(1)}, bf16[2,128,256]{2,1,0:T(8,128)(2,1)S(1)}, u32[]{:S(2)}, u32[]{:S(2)}) collective-permute-start(bf16[2,128,256]{2,1,0:T(8,128)(2,1)S(1)} %get-tuple-element.75), channel_id=1, source_target_pairs={{0,6},{2,0},{4,2},{6,4},{1,7},{3,1},{5,3},{7,5},{8,14},{10,8},{12,... | collective-permute-start | bytes 393224 | tf_op jit(solution)/shard_map/ppermute | solution.py:363
  22.1 0.0 collective-permute-done.5
  22.1 0.0 collective-permute-done.4
  22.1 2.0 %collective-permute-start.7 = (bf16[4,32,256]{2,1,0:T(8,128)(2,1)S(1)}, bf16[4,32,256]{2,1,0:T(8,128)(2,1)S(1)}, u32[]{:S(2)}, u32[]{:S(2)}) collective-permute-start(bf16[4,32,256]{2,1,0:T(8,128)(2,1)S(1)} %get-tuple-element.123), channel_id=1, source_target_pairs={{0,16},{16,0},{1,17},{17,1},{2,18},{18,2},{3,19},{19,3},{4,20},{20... | collective-permute-start | bytes 196616 | tf_op jit(solution)/shard_map/ppermute | solution.py:367
  24.1 1.2 copy-done
  25.3 1.2 copy-done.1
  26.6 1.7 %shard_map.128 = (bf16[4,128,1024]{2,1,0:T(8,128)(2,1)}, bf16[128,1024]{1,0:T(8,128)(2,1)S(1)}, bf16[128,1024]{1,0:T(8,128)(2,1)}, bf16[128,1024]{1,0:T(8,128)(2,1)S(1)}, bf16[128,1024]{1,0:T(8,128)(2,1)S(1)}) custom-call(s32[5]{0:T(128)S(1)} %stack.59.pos_ref, bf16[1,2,128,2048]{3,2,1,0:T(8,128)(2,1)S(1)} %copy-done, bf16[1,2,128,2048]{3,2,1,0:T(8,128)(2,1)S(1)} %copy-done.1), custom_call_target="tpu_custom_call" | custom-call | bytes 4194324 | tf_op jit(solution)/shard_map/pallas_call | solution.py:347
  28.4 0.0 collective-permute-done.1
  28.4 0.0 collective-permute-done.2
  28.5 0.0 copy-start.5
  28.5 2.0 %collective-permute-start.8 = (bf16[1280,256]{1,0:T(8,128)(2,1)S(1)}, bf16[1280,256]{1,0:T(8,128)(2,1)S(1)}, u32[]{:S(2)}, u32[]{:S(2)}) collective-permute-start(bf16[1280,256]{1,0:T(8,128)(2,1)S(1)} %fusion.4.rest_1_.rest_4_), channel_id=1, source_target_pairs={{0,8},{8,0},{1,9},{9,1},{2,10},{10,2},{3,11},{11,3},{4,12},{12,4},... | collective-permute-start | bytes 1966088 | tf_op jit(solution)/shard_map/ppermute | solution.py:367
  30.5 6.2 %all-to-all-start = ((bf16[4,128,1024]{2,1,0:T(8,128)(2,1)}), bf16[4,128,1024]{2,1,0:T(8,128)(2,1)S(1)}, u32[]{:S(2)}, u32[]{:S(2)}) async-start(bf16[4,128,1024]{2,1,0:T(8,128)(2,1)} %get-tuple-element.81), calls=%async_computation | async-start | bytes 2097152 | tf_op jit(solution)/shard_map/all_to_all | solution.py:359
  36.7 7.0 %collective-permute-done.8.rest_3_.rest_6_ = bf16[1280,256]{1,0:T(8,128)(2,1)S(1)} collective-permute-done((bf16[1280,256]{1,0:T(8,128)(2,1)S(1)}, bf16[1280,256]{1,0:T(8,128)(2,1)S(1)}, u32[]{:S(2)}, u32[]{:S(2)}) %collective-permute-start.8) | collective-permute-done | bytes 655392 | tf_op jit(solution)/shard_map/ppermute | solution.py:367
  43.7 0.0 collective-permute-start.13
  43.7 0.1 copy.15.ids_ref
  43.8 0.1 collective-permute-start.9
  43.9 4.2 %collective-permute-start.10 = (bf16[128,1024]{1,0:T(8,128)(2,1)S(1)}, bf16[128,1024]{1,0:T(8,128)(2,1)}, u32[]{:S(2)}, u32[]{:S(2)}) collective-permute-start(bf16[128,1024]{1,0:T(8,128)(2,1)S(1)} %get-tuple-element.79), channel_id=1, source_target_pairs={{0,4},{2,6},{4,0},{6,2},{1,5},{3,7},{5,1},{7,3},{8,12},{10,14},{12... | collective-permute-start | bytes 786440 | tf_op jit(solution)/shard_map/ppermute | solution.py:363
  48.1 0.1 collective-permute-start.11
  48.2 0.0 collective-permute-done.12.rest_2_.rest_5_
  48.2 0.0 all-to-all-done.rest_0_
  48.2 19.0 %shard_map.129 = (bf16[128,1024]{1,0:T(8,128)(2,1)S(1)}, bf16[128,1024]{1,0:T(8,128)(2,1)S(1)}, bf16[128,1024]{1,0:T(8,128)(2,1)S(1)}, bf16[128,1024]{1,0:T(8,12...) custom-call(s32[5]{0:T(128)S(1)} %stack.59.pos_ref, ...), custom_call_target="tpu_custom_call" | custom-call | flops 24999999488 | bytes 6291456 | tf_op jit(solution)/shard_map/pallas_call | solution.py:260
  67.2 1.2 collective-permute-start.14
  68.4 2.3 %collective-permute-start.15 = (bf16[128,1024]{1,0:T(8,128)(2,1)S(1)}, bf16[128,1024]{1,0:T(8,128)(2,1)S(1)}, u32[]{:S(2)}, u32[]{:S(2)}) collective-permute-start(bf16[128,1024]{1,0:T(8,128)(2,1)S(1)} %get-tuple-element.91), channel_id=1, source_target_pairs={{0,4},{2,6},{4,0},{6,2},{1,5},{3,7},{5,1},{7,3},{8,12},{10,14},{12... | collective-permute-start | bytes 786440 | tf_op jit(solution)/shard_map/ppermute | solution.py:363
  70.7 0.1 collective-permute-start.16
  70.8 9.8 %collective-permute-start.17 = (bf16[2,4,128,256]{3,2,1,0:T(8,128)(2,1)S(1)}, bf16[2,4,128,256]{3,2,1,0:T(8,128)(2,1)S(1)}, u32[]{:S(2)}, u32[]{:S(2)}) collective-permute-start(bf16[2,4,128,256]{3,2,1,0:T(8,128)(2,1)S(1)} %get-tuple-element.93), channel_id=1, source_target_pairs={{0,8},{8,0},{1,9},{9,1},{2,10},{10,2},{3,11},{11,3},{4,12},{12,4},... | collective-permute-start | bytes 1572872 | tf_op jit(solution)/shard_map/ppermute | solution.py:367
  80.6 18.0 %shard_map.130 = (bf16[128,1024]{1,0:T(8,128)(2,1)S(1)}, bf16[128,1024]{1,0:T(8,128)(2,1)}, bf16[128,1024]{1,0:T(8,128)(2,1)}, bf16[128,1024]{1,0:T(8,128)(2,1)S...) custom-call(s32[5]{0:T(128)S(1)} %stack.59.pos_ref, ...), custom_call_target="tpu_custom_call" | custom-call | flops 24999999488 | bytes 6291456 | tf_op jit(solution)/shard_map/pallas_call | solution.py:260
  98.7 0.1 collective-permute-start.22
  98.8 0.1 add_convert_fusion.1
  99.0 0.8 collective-permute-start.21
  99.8 0.9 collective-permute-done.22
  100.7 0.1 add_convert_fusion
  100.8 0.7 slice_bitcast_fusion.2
  101.6 7.3 %collective-permute-start.23 = (bf16[4,128,256]{2,1,0:T(8,128)(2,1)}, bf16[4,128,256]{2,1,0:T(8,128)(2,1)}, u32[]{:S(2)}, u32[]{:S(2)}) collective-permute-start(bf16[4,128,256]{2,1,0:T(8,128)(2,1)} %slice_bitcast_fusion.2), channel_id=1, source_target_pairs={{0,8},{8,0},{1,9},{9,1},{2,10},{10,2},{3,11},{11,3},{4,12},{12,4},... | collective-permute-start | bytes 786440 | tf_op jit(solution)/shard_map/ppermute | solution.py:367
  108.8 1.7 %collective-permute-start.18 = (bf16[128,1024]{1,0:T(8,128)(2,1)}, bf16[128,1024]{1,0:T(8,128)(2,1)S(1)}, u32[]{:S(2)}, u32[]{:S(2)}) collective-permute-start(bf16[128,1024]{1,0:T(8,128)(2,1)} %get-tuple-element.99), channel_id=1, source_target_pairs={{0,6},{2,0},{4,2},{6,4},{1,7},{3,1},{5,3},{7,5},{8,14},{10,8},{12,... | collective-permute-start | bytes 786440 | tf_op jit(solution)/shard_map/ppermute | solution.py:363
  110.5 1.4 %collective-permute-start.19 = (bf16[128,1024]{1,0:T(8,128)(2,1)}, bf16[128,1024]{1,0:T(8,128)(2,1)S(1)}, u32[]{:S(2)}, u32[]{:S(2)}) collective-permute-start(bf16[128,1024]{1,0:T(8,128)(2,1)} %get-tuple-element.100), channel_id=1, source_target_pairs={{0,4},{2,6},{4,0},{6,2},{1,5},{3,7},{5,1},{7,3},{8,12},{10,14},{12... | collective-permute-start | bytes 786440 | tf_op jit(solution)/shard_map/ppermute | solution.py:363
  111.9 2.4 %collective-permute-start.20 = (bf16[128,1024]{1,0:T(8,128)(2,1)S(1)}, bf16[128,1024]{1,0:T(8,128)(2,1)S(1)}, u32[]{:S(2)}, u32[]{:S(2)}) collective-permute-start(bf16[128,1024]{1,0:T(8,128)(2,1)S(1)} %get-tuple-element.101), channel_id=1, source_target_pairs={{0,2},{2,4},{4,6},{6,0},{1,3},{3,5},{5,7},{7,1},{8,10},{10,12},{12... | collective-permute-start | bytes 786440 | tf_op jit(solution)/shard_map/ppermute | solution.py:363
  114.3 0.1 fusion.2
  114.4 4.4 %all-to-all-start.1 = ((bf16[32,2,32,128]{3,2,1,0:T(8,128)(2,1)}), bf16[32,2,32,128]{3,2,1,0:T(8,128)(2,1)}, u32[]{:S(2)}, u32[]{:S(2)}) async-start(bf16[32,2,32,128]{3,2,1,0:T(8,128)(2,1)} %bitcast.32), calls=%async_computation.1 | async-start | bytes 1048576 | tf_op jit(solution)/shard_map/all_to_all | solution.py:413
  118.8 1.0 fusion.3
  119.8 0.1 pad_maximum_fusion
  119.9 3.9 %collective-permute-done.19.refs_6_ = bf16[128,1024]{1,0:T(8,128)(2,1)S(1)} collective-permute-done((bf16[128,1024]{1,0:T(8,128)(2,1)}, bf16[128,1024]{1,0:T(8,128)(2,1)S(1)}, u32[]{:S(2)}, u32[]{:S(2)}) %collective-permute-start.19) | collective-permute-done | bytes 262176 | tf_op jit(solution)/shard_map/ppermute | solution.py:363
  123.8 0.9 collective-permute-done.20.refs_7_
  124.8 1.5 %collective-permute-start.26 = (bf16[2,128,256]{2,1,0:T(8,128)(2,1)S(1)}, bf16[2,128,256]{2,1,0:T(8,128)(2,1)S(1)}, u32[]{:S(2)}, u32[]{:S(2)}) collective-permute-start(bf16[2,128,256]{2,1,0:T(8,128)(2,1)S(1)} %get-tuple-element.118), channel_id=1, source_target_pairs={{0,2},{2,4},{4,6},{6,0},{1,3},{3,5},{5,7},{7,1},{8,10},{10,12},{12... | collective-permute-start | bytes 393224 | tf_op jit(solution)/shard_map/ppermute | solution.py:363
  126.3 3.4 %collective-permute-start.25 = (bf16[2,128,256]{2,1,0:T(8,128)(2,1)S(1)}, bf16[2,128,256]{2,1,0:T(8,128)(2,1)S(1)}, u32[]{:S(2)}, u32[]{:S(2)}) collective-permute-start(bf16[2,128,256]{2,1,0:T(8,128)(2,1)S(1)} %get-tuple-element.119), channel_id=1, source_target_pairs={{0,4},{2,6},{4,0},{6,2},{1,5},{3,7},{5,1},{7,3},{8,12},{10,14},{12... | collective-permute-start | bytes 393224 | tf_op jit(solution)/shard_map/ppermute | solution.py:363
  129.6 0.5 collective-permute-start.24
  130.1 1.1 convert_reduce_fusion
  131.3 3.4 %collective-permute-start.27 = (f32[2,32,128]{2,1,0:T(8,128)S(1)}, f32[2,32,128]{2,1,0:T(8,128)S(1)}, u32[]{:S(2)}, u32[]{:S(2)}) collective-permute-start(f32[2,32,128]{2,1,0:T(8,128)S(1)} %convert_reduce_fusion), channel_id=1, source_target_pairs={{0,0},{1,1},{8,2},{9,3},{2,4},{3,5},{10,6},{11,7},{4,8},{5,9},{12,... | collective-permute-start | bytes 98312 | tf_op jit(solution)/shard_map/ppermute | solution.py:422
  134.7 2.0 %shard_map.131 = (bf16[1,2,128,2048]{3,2,1,0:T(8,128)(2,1)}, bf16[1,2,128,2048]{3,2,1,0:T(8,128)(2,1)}) custom-call(s32[5]{0:T(128)S(1)} %stack.59.pos_ref, bf16[128,1024]{1,0:T(8,128)(2,1)S(1)} %get-tuple-element.94.refs_0_, bf16[128,1024]{1,0:T(8,128)(2,1)S(1)} %collective-permute-done.14.refs_1_, bf16[128,1024]{1,0:T(8,128)(2,1)S(1)} %collective-permute-done.15.refs_2_, ...), custom_call_target="tpu_custom_call" | custom-call | bytes 4194324 | tf_op jit(solution)/shard_map/pallas_call | solution.py:347
  136.7 1.4 %shard_map.132 = (bf16[1,2,128,512]{3,2,1,0:T(8,128)(2,1)}, bf16[1,2,128,512]{3,2,1,0:T(8,128)(2,1)}) custom-call(s32[5]{0:T(128)S(1)} %stack.59.pos_ref, bf16[2,128,256]{2,1,0:T(8,128)(2,1)S(1)} %get-tuple-element.121.p0, bf16[2,128,256]{2,1,0:T(8,128)(2,1)S(1)} %collective-permute-done.24.p1, bf16[2,128,256]{2,1,0:T(8,128)(2,1)S(1)} %collective-permute-done.25.p2, ...), custom_call_target="tpu_custom_call" | custom-call | bytes 1048596 | tf_op jit(solution)/shard_map/pallas_call | solution.py:347
  138.1 1.3 collective-permute-done.27
  139.5 0.6 slice_bitcast_fusion.13
  (38 shorter events, 0.2 us)
Async XLA Ops:
  1.4 7.1 %collective-permute-start.3 = (bf16[32,256]{1,0:T(8,128)(2,1)S(1)}, bf16[32,256]{1,0:T(8,128)(2,1)S(1)}, u32[]{:S(2)}, u32[]{:S(2)}) collective-permute-start(bf16[32,256]{1,0:T(8,128)(2,1)S(1)} %pad_maximum_fusion.3), channel_id=1, source_target_pairs={{0,0},{1,1},{2,8},{3,9},{4,2},{5,3},{6,10},{7,11},{8,4},{9,5},{10,... | collective-permute-start | bytes 49160 | tf_op jit(solution)/shard_map/ppermute | solution.py:383
  8.4 11.5 %collective-permute-start.6 = (bf16[32,256]{1,0:T(8,128)(2,1)S(1)}, bf16[32,256]{1,0:T(8,128)(2,1)S(1)}, u32[]{:S(2)}, u32[]{:S(2)}) collective-permute-start(bf16[32,256]{1,0:T(8,128)(2,1)S(1)} %collective-permute-done.3), channel_id=1, source_target_pairs={{0,96},{32,0},{64,32},{96,64},{1,97},{33,1},{65,33},{97,65},{2,98}... | collective-permute-start | bytes 49160 | tf_op jit(solution)/shard_map/ppermute | solution.py:384
  9.0 13.1 %collective-permute-start.5 = (bf16[32,256]{1,0:T(8,128)(2,1)S(1)}, bf16[32,256]{1,0:T(8,128)(2,1)S(1)}, u32[]{:S(2)}, u32[]{:S(2)}) collective-permute-start(bf16[32,256]{1,0:T(8,128)(2,1)S(1)} %collective-permute-done.3), channel_id=1, source_target_pairs={{0,64},{32,96},{64,0},{96,32},{1,65},{33,97},{65,1},{97,33},{2,66}... | collective-permute-start | bytes 49160 | tf_op jit(solution)/shard_map/ppermute | solution.py:384
  11.4 10.7 %collective-permute-start.4 = (bf16[32,256]{1,0:T(8,128)(2,1)S(1)}, bf16[32,256]{1,0:T(8,128)(2,1)S(1)}, u32[]{:S(2)}, u32[]{:S(2)}) collective-permute-start(bf16[32,256]{1,0:T(8,128)(2,1)S(1)} %collective-permute-done.3), channel_id=1, source_target_pairs={{0,32},{32,64},{64,96},{96,0},{1,33},{33,65},{65,97},{97,1},{2,34}... | collective-permute-start | bytes 49160 | tf_op jit(solution)/shard_map/ppermute | solution.py:384
  13.3 1.0 copy-start.2
  14.2 0.9 copy-start.3
  15.8 12.5 %collective-permute-start = (bf16[2,128,256]{2,1,0:T(8,128)(2,1)S(1)}, bf16[2,128,256]{2,1,0:T(8,128)(2,1)S(1)}, u32[]{:S(2)}, u32[]{:S(2)}) collective-permute-start(bf16[2,128,256]{2,1,0:T(8,128)(2,1)S(1)} %get-tuple-element.73), channel_id=1, source_target_pairs={{0,2},{2,4},{4,6},{6,0},{1,3},{3,5},{5,7},{7,1},{8,10},{10,12},{12... | collective-permute-start | bytes 393224 | tf_op jit(solution)/shard_map/ppermute | solution.py:363
  19.9 8.4 %collective-permute-start.1 = (bf16[2,128,256]{2,1,0:T(8,128)(2,1)S(1)}, bf16[2,128,256]{2,1,0:T(8,128)(2,1)S(1)}, u32[]{:S(2)}, u32[]{:S(2)}) collective-permute-start(bf16[2,128,256]{2,1,0:T(8,128)(2,1)S(1)} %get-tuple-element.74), channel_id=1, source_target_pairs={{0,4},{2,6},{4,0},{6,2},{1,5},{3,7},{5,1},{7,3},{8,12},{10,14},{12... | collective-permute-start | bytes 393224 | tf_op jit(solution)/shard_map/ppermute | solution.py:363
  19.9 8.5 %collective-permute-start.2 = (bf16[2,128,256]{2,1,0:T(8,128)(2,1)S(1)}, bf16[2,128,256]{2,1,0:T(8,128)(2,1)S(1)}, u32[]{:S(2)}, u32[]{:S(2)}) collective-permute-start(bf16[2,128,256]{2,1,0:T(8,128)(2,1)S(1)} %get-tuple-element.75), channel_id=1, source_target_pairs={{0,6},{2,0},{4,2},{6,4},{1,7},{3,1},{5,3},{7,5},{8,14},{10,8},{12,... | collective-permute-start | bytes 393224 | tf_op jit(solution)/shard_map/ppermute | solution.py:363
  22.1 6.2 %collective-permute-start.7 = (bf16[4,32,256]{2,1,0:T(8,128)(2,1)S(1)}, bf16[4,32,256]{2,1,0:T(8,128)(2,1)S(1)}, u32[]{:S(2)}, u32[]{:S(2)}) collective-permute-start(bf16[4,32,256]{2,1,0:T(8,128)(2,1)S(1)} %get-tuple-element.123), channel_id=1, source_target_pairs={{0,16},{16,0},{1,17},{17,1},{2,18},{18,2},{3,19},{19,3},{4,20},{20... | collective-permute-start | bytes 196616 | tf_op jit(solution)/shard_map/ppermute | solution.py:367
  24.1 1.2 copy-start
  25.3 1.2 copy-start.1
  28.5 15.2 %copy-start.5 = (s32[8,2]{0,1:T(2,128)S(1)}, s32[8,2]{0,1:T(2,128)}, u32[]{:S(2)}) copy-start(s32[8,2]{0,1:T(2,128)} %param.15) | copy-start | bytes 196
  28.5 15.2 %collective-permute-start.8 = (bf16[1280,256]{1,0:T(8,128)(2,1)S(1)}, bf16[1280,256]{1,0:T(8,128)(2,1)S(1)}, u32[]{:S(2)}, u32[]{:S(2)}) collective-permute-start(bf16[1280,256]{1,0:T(8,128)(2,1)S(1)} %fusion.4.rest_1_.rest_4_), channel_id=1, source_target_pairs={{0,8},{8,0},{1,9},{9,1},{2,10},{10,2},{3,11},{11,3},{4,12},{12,4},... | collective-permute-start | bytes 1966088 | tf_op jit(solution)/shard_map/ppermute | solution.py:367
  30.5 17.8 %all-to-all-start = ((bf16[4,128,1024]{2,1,0:T(8,128)(2,1)}), bf16[4,128,1024]{2,1,0:T(8,128)(2,1)S(1)}, u32[]{:S(2)}, u32[]{:S(2)}) async-start(bf16[4,128,1024]{2,1,0:T(8,128)(2,1)} %get-tuple-element.81), calls=%async_computation | async-start | bytes 2097152 | tf_op jit(solution)/shard_map/all_to_all | solution.py:359
  36.7 11.5 %collective-permute-start.12 = (bf16[1280,256]{1,0:T(8,128)(2,1)S(1)}, bf16[1280,256]{1,0:T(8,128)(2,1)}, u32[]{:S(2)}, u32[]{:S(2)}) collective-permute-start(bf16[1280,256]{1,0:T(8,128)(2,1)S(1)} %fusion.4.rest_1_.rest_4_), channel_id=1, source_target_pairs={{0,1},{1,0},{2,3},{3,2},{4,5},{5,4},{6,7},{7,6},{8,9},{9,8},{10,11... | collective-permute-start | bytes 1966088 | tf_op jit(solution)/shard_map/ppermute | solution.py:367
  43.7 4.5 %collective-permute-start.13 = (bf16[1280,256]{1,0:T(8,128)(2,1)S(1)}, bf16[1280,256]{1,0:T(8,128)(2,1)}, u32[]{:S(2)}, u32[]{:S(2)}) collective-permute-start(bf16[1280,256]{1,0:T(8,128)(2,1)S(1)} %collective-permute-done.8.rest_3_.rest_6_), channel_id=1, source_target_pairs={{0,1},{1,0},{2,3},{3,2},{4,5},{5,4},{6,7},{7,6},{8,9},{9,8},{10,11... | collective-permute-start | bytes 1966088 | tf_op jit(solution)/shard_map/ppermute | solution.py:367
  43.8 4.4 %copy-start.4 = (s32[8]{0:T(128)S(1)}, s32[8]{0:T(128)}, u32[]{:S(2)}) copy-start(s32[8]{0:T(128)} %cnt_ref.3) | copy-start | bytes 100
  43.8 26.9 %collective-permute-start.9 = (bf16[128,1024]{1,0:T(8,128)(2,1)}, bf16[128,1024]{1,0:T(8,128)(2,1)}, u32[]{:S(2)}, u32[]{:S(2)}) collective-permute-start(bf16[128,1024]{1,0:T(8,128)(2,1)} %get-tuple-element.78), channel_id=1, source_target_pairs={{0,2},{2,4},{4,6},{6,0},{1,3},{3,5},{5,7},{7,1},{8,10},{10,12},{12... | collective-permute-start | bytes 786440 | tf_op jit(solution)/shard_map/ppermute | solution.py:363
  43.9 26.9 %collective-permute-start.10 = (bf16[128,1024]{1,0:T(8,128)(2,1)S(1)}, bf16[128,1024]{1,0:T(8,128)(2,1)}, u32[]{:S(2)}, u32[]{:S(2)}) collective-permute-start(bf16[128,1024]{1,0:T(8,128)(2,1)S(1)} %get-tuple-element.79), channel_id=1, source_target_pairs={{0,4},{2,6},{4,0},{6,2},{1,5},{3,7},{5,1},{7,3},{8,12},{10,14},{12... | collective-permute-start | bytes 786440 | tf_op jit(solution)/shard_map/ppermute | solution.py:363
  48.1 32.5 %collective-permute-start.11 = (bf16[128,1024]{1,0:T(8,128)(2,1)S(1)}, bf16[128,1024]{1,0:T(8,128)(2,1)}, u32[]{:S(2)}, u32[]{:S(2)}) collective-permute-start(bf16[128,1024]{1,0:T(8,128)(2,1)S(1)} %get-tuple-element.80), channel_id=1, source_target_pairs={{0,6},{2,0},{4,2},{6,4},{1,7},{3,1},{5,3},{7,5},{8,14},{10,8},{12,... | collective-permute-start | bytes 786440 | tf_op jit(solution)/shard_map/ppermute | solution.py:363
  67.2 31.5 %collective-permute-start.14 = (bf16[128,1024]{1,0:T(8,128)(2,1)S(1)}, bf16[128,1024]{1,0:T(8,128)(2,1)S(1)}, u32[]{:S(2)}, u32[]{:S(2)}) collective-permute-start(bf16[128,1024]{1,0:T(8,128)(2,1)S(1)} %get-tuple-element.90), channel_id=1, source_target_pairs={{0,6},{2,0},{4,2},{6,4},{1,7},{3,1},{5,3},{7,5},{8,14},{10,8},{12,... | collective-permute-start | bytes 786440 | tf_op jit(solution)/shard_map/ppermute | solution.py:363
  68.4 30.3 %collective-permute-start.15 = (bf16[128,1024]{1,0:T(8,128)(2,1)S(1)}, bf16[128,1024]{1,0:T(8,128)(2,1)S(1)}, u32[]{:S(2)}, u32[]{:S(2)}) collective-permute-start(bf16[128,1024]{1,0:T(8,128)(2,1)S(1)} %get-tuple-element.91), channel_id=1, source_target_pairs={{0,4},{2,6},{4,0},{6,2},{1,5},{3,7},{5,1},{7,3},{8,12},{10,14},{12... | collective-permute-start | bytes 786440 | tf_op jit(solution)/shard_map/ppermute | solution.py:363
  70.7 27.9 %collective-permute-start.16 = (bf16[128,1024]{1,0:T(8,128)(2,1)S(1)}, bf16[128,1024]{1,0:T(8,128)(2,1)S(1)}, u32[]{:S(2)}, u32[]{:S(2)}) collective-permute-start(bf16[128,1024]{1,0:T(8,128)(2,1)S(1)} %get-tuple-element.92), channel_id=1, source_target_pairs={{0,2},{2,4},{4,6},{6,0},{1,3},{3,5},{5,7},{7,1},{8,10},{10,12},{12... | collective-permute-start | bytes 786440 | tf_op jit(solution)/shard_map/ppermute | solution.py:363
  70.8 27.9 %collective-permute-start.17 = (bf16[2,4,128,256]{3,2,1,0:T(8,128)(2,1)S(1)}, bf16[2,4,128,256]{3,2,1,0:T(8,128)(2,1)S(1)}, u32[]{:S(2)}, u32[]{:S(2)}) collective-permute-start(bf16[2,4,128,256]{3,2,1,0:T(8,128)(2,1)S(1)} %get-tuple-element.93), channel_id=1, source_target_pairs={{0,8},{8,0},{1,9},{9,1},{2,10},{10,2},{3,11},{11,3},{4,12},{12,4},... | collective-permute-start | bytes 1572872 | tf_op jit(solution)/shard_map/ppermute | solution.py:367
  98.7 2.0 %collective-permute-start.22 = (bf16[2,4,128,256]{3,2,1,0:T(8,128)(2,1)S(1)}, bf16[2,4,128,256]{3,2,1,0:T(8,128)(2,1)S(1)}, u32[]{:S(2)}, u32[]{:S(2)}) collective-permute-start(bf16[2,4,128,256]{3,2,1,0:T(8,128)(2,1)S(1)} %get-tuple-element.106), channel_id=1, source_target_pairs={{0,1},{1,0},{2,3},{3,2},{4,5},{5,4},{6,7},{7,6},{8,9},{9,8},{10,11... | collective-permute-start | bytes 1572872 | tf_op jit(solution)/shard_map/ppermute | solution.py:367
  99.0 15.3 %collective-permute-start.21 = (bf16[4,128,256]{2,1,0:T(8,128)(2,1)S(1)}, bf16[4,128,256]{2,1,0:T(8,128)(2,1)S(1)}, u32[]{:S(2)}, u32[]{:S(2)}) collective-permute-start(bf16[4,128,256]{2,1,0:T(8,128)(2,1)S(1)} %slice_bitcast_fusion), channel_id=1, source_target_pairs={{0,1},{1,0},{2,3},{3,2},{4,5},{5,4},{6,7},{7,6},{8,9},{9,8},{10,11... | collective-permute-start | bytes 786440 | tf_op jit(solution)/shard_map/ppermute | solution.py:367
  101.6 17.2 %collective-permute-start.23 = (bf16[4,128,256]{2,1,0:T(8,128)(2,1)}, bf16[4,128,256]{2,1,0:T(8,128)(2,1)}, u32[]{:S(2)}, u32[]{:S(2)}) collective-permute-start(bf16[4,128,256]{2,1,0:T(8,128)(2,1)} %slice_bitcast_fusion.2), channel_id=1, source_target_pairs={{0,8},{8,0},{1,9},{9,1},{2,10},{10,2},{3,11},{11,3},{4,12},{12,4},... | collective-permute-start | bytes 786440 | tf_op jit(solution)/shard_map/ppermute | solution.py:367
  108.8 11.1 %collective-permute-start.18 = (bf16[128,1024]{1,0:T(8,128)(2,1)}, bf16[128,1024]{1,0:T(8,128)(2,1)S(1)}, u32[]{:S(2)}, u32[]{:S(2)}) collective-permute-start(bf16[128,1024]{1,0:T(8,128)(2,1)} %get-tuple-element.99), channel_id=1, source_target_pairs={{0,6},{2,0},{4,2},{6,4},{1,7},{3,1},{5,3},{7,5},{8,14},{10,8},{12,... | collective-permute-start | bytes 786440 | tf_op jit(solution)/shard_map/ppermute | solution.py:363
  110.5 13.3 %collective-permute-start.19 = (bf16[128,1024]{1,0:T(8,128)(2,1)}, bf16[128,1024]{1,0:T(8,128)(2,1)S(1)}, u32[]{:S(2)}, u32[]{:S(2)}) collective-permute-start(bf16[128,1024]{1,0:T(8,128)(2,1)} %get-tuple-element.100), channel_id=1, source_target_pairs={{0,4},{2,6},{4,0},{6,2},{1,5},{3,7},{5,1},{7,3},{8,12},{10,14},{12... | collective-permute-start | bytes 786440 | tf_op jit(solution)/shard_map/ppermute | solution.py:363
  111.9 12.8 %collective-permute-start.20 = (bf16[128,1024]{1,0:T(8,128)(2,1)S(1)}, bf16[128,1024]{1,0:T(8,128)(2,1)S(1)}, u32[]{:S(2)}, u32[]{:S(2)}) collective-permute-start(bf16[128,1024]{1,0:T(8,128)(2,1)S(1)} %get-tuple-element.101), channel_id=1, source_target_pairs={{0,2},{2,4},{4,6},{6,0},{1,3},{3,5},{5,7},{7,1},{8,10},{10,12},{12... | collective-permute-start | bytes 786440 | tf_op jit(solution)/shard_map/ppermute | solution.py:363
  114.4 15.8 %all-to-all-start.1 = ((bf16[32,2,32,128]{3,2,1,0:T(8,128)(2,1)}), bf16[32,2,32,128]{3,2,1,0:T(8,128)(2,1)}, u32[]{:S(2)}, u32[]{:S(2)}) async-start(bf16[32,2,32,128]{3,2,1,0:T(8,128)(2,1)} %bitcast.32), calls=%async_computation.1 | async-start | bytes 1048576 | tf_op jit(solution)/shard_map/all_to_all | solution.py:413
  124.8 11.9 %collective-permute-start.26 = (bf16[2,128,256]{2,1,0:T(8,128)(2,1)S(1)}, bf16[2,128,256]{2,1,0:T(8,128)(2,1)S(1)}, u32[]{:S(2)}, u32[]{:S(2)}) collective-permute-start(bf16[2,128,256]{2,1,0:T(8,128)(2,1)S(1)} %get-tuple-element.118), channel_id=1, source_target_pairs={{0,2},{2,4},{4,6},{6,0},{1,3},{3,5},{5,7},{7,1},{8,10},{10,12},{12... | collective-permute-start | bytes 393224 | tf_op jit(solution)/shard_map/ppermute | solution.py:363
  126.3 10.4 %collective-permute-start.25 = (bf16[2,128,256]{2,1,0:T(8,128)(2,1)S(1)}, bf16[2,128,256]{2,1,0:T(8,128)(2,1)S(1)}, u32[]{:S(2)}, u32[]{:S(2)}) collective-permute-start(bf16[2,128,256]{2,1,0:T(8,128)(2,1)S(1)} %get-tuple-element.119), channel_id=1, source_target_pairs={{0,4},{2,6},{4,0},{6,2},{1,5},{3,7},{5,1},{7,3},{8,12},{10,14},{12... | collective-permute-start | bytes 393224 | tf_op jit(solution)/shard_map/ppermute | solution.py:363
  129.6 7.1 %collective-permute-start.24 = (bf16[2,128,256]{2,1,0:T(8,128)(2,1)S(1)}, bf16[2,128,256]{2,1,0:T(8,128)(2,1)S(1)}, u32[]{:S(2)}, u32[]{:S(2)}) collective-permute-start(bf16[2,128,256]{2,1,0:T(8,128)(2,1)S(1)} %get-tuple-element.120), channel_id=1, source_target_pairs={{0,6},{2,0},{4,2},{6,4},{1,7},{3,1},{5,3},{7,5},{8,14},{10,8},{12,... | collective-permute-start | bytes 393224 | tf_op jit(solution)/shard_map/ppermute | solution.py:363
  131.3 8.2 %collective-permute-start.27 = (f32[2,32,128]{2,1,0:T(8,128)S(1)}, f32[2,32,128]{2,1,0:T(8,128)S(1)}, u32[]{:S(2)}, u32[]{:S(2)}) collective-permute-start(f32[2,32,128]{2,1,0:T(8,128)S(1)} %convert_reduce_fusion), channel_id=1, source_target_pairs={{0,0},{1,1},{8,2},{9,3},{2,4},{3,5},{10,6},{11,7},{4,8},{5,9},{12,... | collective-permute-start | bytes 98312 | tf_op jit(solution)/shard_map/ppermute | solution.py:422
where the time goes:
time: 140 us
  starting transfers between devices  71.5 us (51%)
  Pallas kernels  42.8 us (31%)
  waiting for transfers between devices  15.6 us (11%)
  local copies, waits for them, and re-layouts  5.97 us (4%)
  other arithmetic  3.3 us (2%)
    pallas_call x2, Pallas kernels, span_call(): pl.pallas_call(functools.partial(span_kernel, ordinal), out_shape=out + (...  37 us
    ppermute x15, starting transfers between devices, y_shift(): return lax.ppermute(a, 'y', [(i, (i + sh) % 4) for i in range(4)])  25.1 us
    ppermute x8, starting transfers between devices, flip(): return lax.ppermute(a, axis, [(0, 1), (1, 0)])  21.9 us
    ppermute x8, waiting for transfers between devices, flip(): return lax.ppermute(a, axis, [(0, 1), (1, 0)])  7.93 us
    all_to_all x1, starting transfers between devices, y_exchange(): return lax.all_to_all(a, 'y', split_axis=0, concat_axis=0, tiled=True)  6.25 us
    pallas_call x4, Pallas kernels, relayout(): pl.pallas_call(kernel, out_shape=tuple((jax.ShapeDtypeStruct(o, BF) for o...  5.78 us
    ppermute x1, starting transfers between devices, per_device(): cache = lax.ppermute(cache, SP, perm)  5.66 us
    ppermute x15, waiting for transfers between devices, y_shift(): return lax.ppermute(a, 'y', [(i, (i + sh) % 4) for i in range(4)])  4.87 us
  transfers between devices with their start and end apart: 30, of which 6 were waited for; matrix products, arithmetic and copies ran while one was open for 3% of the time, Pallas kernels for 31%

commit v1 on v0

--- a/solution.py
+++ b/solution.py
@@ -405,16 +405,18 @@
     back0 = [out0[0]] + [y_shift(out0[sh], 4 - sh) for sh in (1, 2, 3)]
     got0 = flip(send0, "zhi")
     (out1, send1, hg, back0, got0) = lax.optimization_barrier((out1, send1, hg, back0, got0))
-    sum0 = (keep0.astype(F32) + got0.astype(F32)).astype(BF)
+    here0 = keep0[0].astype(F32) + got0[0].astype(F32)
+    away0 = (keep0[1].astype(F32) + got0[1].astype(F32)).astype(BF)
     got1 = flip(send1, "core")
     back1 = [out1[0]] + [y_shift(out1[sh], 4 - sh) for sh in (1, 2, 3)]
-    sum1 = (keep1.astype(F32) + got1.astype(F32)).astype(BF)
-    hg, sum1 = lax.optimization_barrier((hg, sum1))
+    here1 = keep1[0].astype(F32) + got1[0].astype(F32)
+    away1 = (keep1[1].astype(F32) + got1[1].astype(F32)).astype(BF)
+    hg, away1 = lax.optimization_barrier((hg, away1))
     hg = lax.all_to_all(hg.reshape(32, 2, 32, TB), FS + ("zhi", "core"), split_axis=0, concat_axis=0, tiled=True)
-    got0 = flip(sum0[1], "core")
-    got1 = flip(sum1[1], "zhi")
-    red0 = sum0[0].astype(F32) + got0.astype(F32)
-    red1 = sum1[0].astype(F32) + got1.astype(F32)
+    got0 = flip(away0, "core")
+    got1 = flip(away1, "zhi")
+    red0 = here0 + got0.astype(F32)
+    red1 = here1 + got1.astype(F32)
     red = jnp.stack([red0, red1], axis=1).astype(BF)
     back1, red = lax.optimization_barrier((back1, red))
     kv_back = [red[0]] + [y_shift(red[sh], 4 - sh) for sh in (1, 2, 3)]

time: 140 us -> 141 us (level)
  the two profiles are of different devices: /device:TPU:10 before, /device:TPU:1 now
where the time goes in v1:
time: 141 us; the launch traced here: 138 us
  starting transfers between devices  69.7 us (49%)
  Pallas kernels  40.4 us (29%)
  waiting for transfers between devices  16.5 us (12%)
  local copies, waits for them, and re-layouts  7.82 us (6%)
  other arithmetic  3.01 us (2%)
    pallas_call x2, Pallas kernels, span_call(): pl.pallas_call(functools.partial(span_kernel, ordinal), out_shape=out + (...  34.7 us
    ppermute x8, starting transfers between devices, flip(): return lax.ppermute(a, axis, [(0, 1), (1, 0)])  31.1 us
    ppermute x15, starting transfers between devices, y_shift(): return lax.ppermute(a, 'y', [(i, (i + sh) % 4) for i in range(4)])  24 us
    ppermute x15, waiting for transfers between devices, y_shift(): return lax.ppermute(a, 'y', [(i, (i + sh) % 4) for i in range(4)])  10.9 us
    unnamed x35, local copies, waits for them, and re-layouts  7.08 us
    pallas_call x4, Pallas kernels, relayout(): pl.pallas_call(kernel, out_shape=tuple((jax.ShapeDtypeStruct(o, BF) for o...  5.7 us
    ppermute x8, waiting for transfers between devices, flip(): return lax.ppermute(a, axis, [(0, 1), (1, 0)])  5.58 us
    all_to_all x1, starting transfers between devices, per_device(): lax.all_to_all(hg.reshape(32, 2, 32, TB), FS + ('zhi', 'core'), split_axi...  5.3 us
  transfers between devices with their start and end apart: 30, of which 5 were waited for; matrix products, arithmetic and copies ran while one was open for 2% of the time, Pallas kernels for 29%

profile of v1, /device:TPU:1, one launch (start us, length us, event | category | flops | bytes accessed | tf_op | source)
XLA Modules:
  0.0 138.5 jit_solution(4781789723981833022)
XLA Ops:
  0.6 0.7 pad_maximum_fusion.3
  1.4 0.7 collective-permute-start.3
  2.0 3.4 %collective-permute-start.6 = (bf16[32,256]{1,0:T(8,128)(2,1)S(1)}, bf16[32,256]{1,0:T(8,128)(2,1)S(1)}, u32[]{:S(2)}, u32[]{:S(2)}) collective-permute-start(bf16[32,256]{1,0:T(8,128)(2,1)S(1)} %collective-permute-done.3), channel_id=1, source_target_pairs={{0,96},{32,0},{64,32},{96,64},{1,97},{33,1},{65,33},{97,65},{2,98}... | collective-permute-start | bytes 49160 | tf_op jit(solution)/shard_map/ppermute | solution.py:384
  5.4 0.5 collective-permute-start.5
  5.9 0.6 collective-permute-start.4
  6.5 0.1 stack.59.pos_ref
  6.6 0.9 copy-done.2
  7.6 0.9 copy-done.3
  8.5 0.6 shard_map.127
  9.2 6.9 %collective-permute-start = (bf16[2,128,256]{2,1,0:T(8,128)(2,1)S(1)}, bf16[2,128,256]{2,1,0:T(8,128)(2,1)S(1)}, u32[]{:S(2)}, u32[]{:S(2)}) collective-permute-start(bf16[2,128,256]{2,1,0:T(8,128)(2,1)S(1)} %get-tuple-element.73), channel_id=1, source_target_pairs={{0,2},{2,4},{4,6},{6,0},{1,3},{3,5},{5,7},{7,1},{8,10},{10,12},{12... | collective-permute-start | bytes 393224 | tf_op jit(solution)/shard_map/ppermute | solution.py:363
  16.0 3.9 %collective-permute-start.1 = (bf16[2,128,256]{2,1,0:T(8,128)(2,1)S(1)}, bf16[2,128,256]{2,1,0:T(8,128)(2,1)S(1)}, u32[]{:S(2)}, u32[]{:S(2)}) collective-permute-start(bf16[2,128,256]{2,1,0:T(8,128)(2,1)S(1)} %get-tuple-element.74), channel_id=1, source_target_pairs={{0,4},{2,6},{4,0},{6,2},{1,5},{3,7},{5,1},{7,3},{8,12},{10,14},{12... | collective-permute-start | bytes 393224 | tf_op jit(solution)/shard_map/ppermute | solution.py:363
  19.9 0.0 collective-permute-done.6
  19.9 2.0 %collective-permute-start.2 = (bf16[2,128,256]{2,1,0:T(8,128)(2,1)S(1)}, bf16[2,128,256]{2,1,0:T(8,128)(2,1)S(1)}, u32[]{:S(2)}, u32[]{:S(2)}) collective-permute-start(bf16[2,128,256]{2,1,0:T(8,128)(2,1)S(1)} %get-tuple-element.75), channel_id=1, source_target_pairs={{0,6},{2,0},{4,2},{6,4},{1,7},{3,1},{5,3},{7,5},{8,14},{10,8},{12,... | collective-permute-start | bytes 393224 | tf_op jit(solution)/shard_map/ppermute | solution.py:363
  21.9 1.7 %collective-permute-start.7 = (bf16[4,32,256]{2,1,0:T(8,128)(2,1)S(1)}, bf16[4,32,256]{2,1,0:T(8,128)(2,1)S(1)}, u32[]{:S(2)}, u32[]{:S(2)}) collective-permute-start(bf16[4,32,256]{2,1,0:T(8,128)(2,1)S(1)} %get-tuple-element.123), channel_id=1, source_target_pairs={{0,16},{16,0},{1,17},{17,1},{2,18},{18,2},{3,19},{19,3},{4,20},{20... | collective-permute-start | bytes 196616 | tf_op jit(solution)/shard_map/ppermute | solution.py:367
  23.6 1.2 copy-done
  24.8 1.2 copy-done.1
  26.1 1.6 %shard_map.128 = (bf16[4,128,1024]{2,1,0:T(8,128)(2,1)}, bf16[128,1024]{1,0:T(8,128)(2,1)S(1)}, bf16[128,1024]{1,0:T(8,128)(2,1)S(1)}, bf16[128,1024]{1,0:T(8,128)(2,1)S(1)}, bf16[128,1024]{1,0:T(8,128)(2,1)S(1)}) custom-call(s32[5]{0:T(128)S(1)} %stack.59.pos_ref, bf16[1,2,128,2048]{3,2,1,0:T(8,128)(2,1)S(1)} %copy-done, bf16[1,2,128,2048]{3,2,1,0:T(8,128)(2,1)S(1)} %copy-done.1), custom_call_target="tpu_custom_call" | custom-call | bytes 4194324 | tf_op jit(solution)/shard_map/pallas_call | solution.py:347
  27.7 0.0 copy-start.8
  27.7 0.0 copy-start.9
  27.7 0.0 collective-permute-done.7
  27.8 0.0 collective-permute-done
  27.9 0.5 copy-done.7
  28.4 0.1 copy-done.8
  28.5 0.1 copy-done.9
  28.6 2.1 %collective-permute-start.8 = (bf16[1280,256]{1,0:T(8,128)(2,1)S(1)}, bf16[1280,256]{1,0:T(8,128)(2,1)S(1)}, u32[]{:S(2)}, u32[]{:S(2)}) collective-permute-start(bf16[1280,256]{1,0:T(8,128)(2,1)S(1)} %fusion.6.rest_1_.rest_4_), channel_id=1, source_target_pairs={{0,8},{8,0},{1,9},{9,1},{2,10},{10,2},{3,11},{11,3},{4,12},{12,4},... | collective-permute-start | bytes 1966088 | tf_op jit(solution)/shard_map/ppermute | solution.py:367
  30.7 3.5 %all-to-all-start = ((bf16[4,128,1024]{2,1,0:T(8,128)(2,1)}), bf16[4,128,1024]{2,1,0:T(8,128)(2,1)S(1)}, u32[]{:S(2)}, u32[]{:S(2)}) async-start(bf16[4,128,1024]{2,1,0:T(8,128)(2,1)} %get-tuple-element.81), calls=%async_computation | async-start | bytes 2097152 | tf_op jit(solution)/shard_map/all_to_all | solution.py:359
  34.2 3.9 %collective-permute-start.12 = (bf16[1280,256]{1,0:T(8,128)(2,1)S(1)}, bf16[1280,256]{1,0:T(8,128)(2,1)S(1)}, u32[]{:S(2)}, u32[]{:S(2)}) collective-permute-start(bf16[1280,256]{1,0:T(8,128)(2,1)S(1)} %fusion.6.rest_1_.rest_4_), channel_id=1, source_target_pairs={{0,1},{1,0},{2,3},{3,2},{4,5},{5,4},{6,7},{7,6},{8,9},{9,8},{10,11... | collective-permute-start | bytes 1966088 | tf_op jit(solution)/shard_map/ppermute | solution.py:367
  38.1 4.5 %collective-permute-done.8.rest_3_.rest_6_ = bf16[1280,256]{1,0:T(8,128)(2,1)S(1)} collective-permute-done((bf16[1280,256]{1,0:T(8,128)(2,1)S(1)}, bf16[1280,256]{1,0:T(8,128)(2,1)S(1)}, u32[]{:S(2)}, u32[]{:S(2)}) %collective-permute-start.8) | collective-permute-done | bytes 655392 | tf_op jit(solution)/shard_map/ppermute | solution.py:367
  42.5 4.7 %collective-permute-start.13 = (bf16[1280,256]{1,0:T(8,128)(2,1)S(1)}, bf16[1280,256]{1,0:T(8,128)(2,1)}, u32[]{:S(2)}, u32[]{:S(2)}) collective-permute-start(bf16[1280,256]{1,0:T(8,128)(2,1)S(1)} %collective-permute-done.8.rest_3_.rest_6_), channel_id=1, source_target_pairs={{0,1},{1,0},{2,3},{3,2},{4,5},{5,4},{6,7},{7,6},{8,9},{9,8},{10,11... | collective-permute-start | bytes 1966088 | tf_op jit(solution)/shard_map/ppermute | solution.py:367
  47.2 0.1 copy.15.ids_ref
  47.3 0.0 collective-permute-start.9
  47.3 1.2 collective-permute-start.10
  48.5 1.5 %collective-permute-start.11 = (bf16[128,1024]{1,0:T(8,128)(2,1)}, bf16[128,1024]{1,0:T(8,128)(2,1)}, u32[]{:S(2)}, u32[]{:S(2)}) collective-permute-start(bf16[128,1024]{1,0:T(8,128)(2,1)} %copy-done.7), channel_id=1, source_target_pairs={{0,6},{2,0},{4,2},{6,4},{1,7},{3,1},{5,3},{7,5},{8,14},{10,8},{12,... | collective-permute-start | bytes 786440 | tf_op jit(solution)/shard_map/ppermute | solution.py:363
  50.0 0.8 copy-done.4
  50.9 1.1 copy-done.5
  52.0 16.8 %shard_map.129 = (bf16[128,1024]{1,0:T(8,128)(2,1)S(1)}, bf16[128,1024]{1,0:T(8,128)(2,1)S(1)}, bf16[128,1024]{1,0:T(8,128)(2,1)S(1)}, bf16[128,1024]{1,0:T(8,12...) custom-call(s32[5]{0:T(128)S(1)} %stack.59.pos_ref, ...), custom_call_target="tpu_custom_call" | custom-call | flops 24999999488 | bytes 6291456 | tf_op jit(solution)/shard_map/pallas_call | solution.py:260
  68.7 0.7 collective-permute-start.14
  69.5 1.8 %collective-permute-start.15 = (bf16[128,1024]{1,0:T(8,128)(2,1)S(1)}, bf16[128,1024]{1,0:T(8,128)(2,1)S(1)}, u32[]{:S(2)}, u32[]{:S(2)}) collective-permute-start(bf16[128,1024]{1,0:T(8,128)(2,1)S(1)} %get-tuple-element.91), channel_id=1, source_target_pairs={{0,4},{2,6},{4,0},{6,2},{1,5},{3,7},{5,1},{7,3},{8,12},{10,14},{12... | collective-permute-start | bytes 786440 | tf_op jit(solution)/shard_map/ppermute | solution.py:363
  71.2 0.8 collective-permute-start.16
  72.0 9.3 %collective-permute-start.17 = (bf16[2,4,128,256]{3,2,1,0:T(8,128)(2,1)S(1)}, bf16[2,4,128,256]{3,2,1,0:T(8,128)(2,1)S(1)}, u32[]{:S(2)}, u32[]{:S(2)}) collective-permute-start(bf16[2,4,128,256]{3,2,1,0:T(8,128)(2,1)S(1)} %get-tuple-element.93), channel_id=1, source_target_pairs={{0,8},{8,0},{1,9},{9,1},{2,10},{10,2},{3,11},{11,3},{4,12},{12,4},... | collective-permute-start | bytes 1572872 | tf_op jit(solution)/shard_map/ppermute | solution.py:367
  81.3 17.9 %shard_map.130 = (bf16[128,1024]{1,0:T(8,128)(2,1)S(1)}, bf16[128,1024]{1,0:T(8,128)(2,1)}, bf16[128,1024]{1,0:T(8,128)(2,1)}, bf16[128,1024]{1,0:T(8,128)(2,1)}...) custom-call(s32[5]{0:T(128)S(1)} %stack.59.pos_ref, ...), custom_call_target="tpu_custom_call" | custom-call | flops 24999999488 | bytes 6291456 | tf_op jit(solution)/shard_map/pallas_call | solution.py:260
  99.3 2.1 %collective-permute-start.22 = (bf16[2,4,128,256]{3,2,1,0:T(8,128)(2,1)S(1)}, bf16[2,4,128,256]{3,2,1,0:T(8,128)(2,1)S(1)}, u32[]{:S(2)}, u32[]{:S(2)}) collective-permute-start(bf16[2,4,128,256]{3,2,1,0:T(8,128)(2,1)S(1)} %get-tuple-element.105), channel_id=1, source_target_pairs={{0,1},{1,0},{2,3},{3,2},{4,5},{5,4},{6,7},{7,6},{8,9},{9,8},{10,11... | collective-permute-start | bytes 1572872 | tf_op jit(solution)/shard_map/ppermute | solution.py:367
  101.4 0.1 fusion.2
  101.4 0.4 collective-permute-start.21
  101.8 1.1 collective-permute-done.22
  102.9 0.8 fusion.3
  103.7 7.0 %collective-permute-start.23 = (bf16[4,128,256]{2,1,0:T(8,128)(2,1)}, bf16[4,128,256]{2,1,0:T(8,128)(2,1)}, u32[]{:S(2)}, u32[]{:S(2)}) collective-permute-start(bf16[4,128,256]{2,1,0:T(8,128)(2,1)} %fusion.3), channel_id=1, source_target_pairs={{0,8},{8,0},{1,9},{9,1},{2,10},{10,2},{3,11},{11,3},{4,12},{12,4},... | collective-permute-start | bytes 786440 | tf_op jit(solution)/shard_map/ppermute | solution.py:367
  110.7 2.0 %collective-permute-start.18 = (bf16[128,1024]{1,0:T(8,128)(2,1)}, bf16[128,1024]{1,0:T(8,128)(2,1)S(1)}, u32[]{:S(2)}, u32[]{:S(2)}) collective-permute-start(bf16[128,1024]{1,0:T(8,128)(2,1)} %get-tuple-element.99), channel_id=1, source_target_pairs={{0,6},{2,0},{4,2},{6,4},{1,7},{3,1},{5,3},{7,5},{8,14},{10,8},{12,... | collective-permute-start | bytes 786440 | tf_op jit(solution)/shard_map/ppermute | solution.py:363
  112.7 0.6 collective-permute-start.20
  113.3 0.1 fusion.4
  113.4 5.3 %all-to-all-start.1 = ((bf16[32,2,32,128]{3,2,1,0:T(8,128)(2,1)}), bf16[32,2,32,128]{3,2,1,0:T(8,128)(2,1)S(1)}, u32[]{:S(2)}, u32[]{:S(2)}) async-start(bf16[32,2,32,128]{3,2,1,0:T(8,128)(2,1)} %bitcast.32), calls=%async_computation.1 | async-start | bytes 1048576 | tf_op jit(solution)/shard_map/all_to_all | solution.py:415
  118.8 1.1 fusion.5
  119.9 0.1 pad_maximum_fusion
  120.0 1.4 %collective-permute-done.19.refs_6_ = bf16[128,1024]{1,0:T(8,128)(2,1)S(1)} collective-permute-done((bf16[128,1024]{1,0:T(8,128)(2,1)}, bf16[128,1024]{1,0:T(8,128)(2,1)S(1)}, u32[]{:S(2)}, u32[]{:S(2)}) %collective-permute-start.19) | collective-permute-done | bytes 262176 | tf_op jit(solution)/shard_map/ppermute | solution.py:363
  121.4 6.2 %collective-permute-done.20.refs_7_ = bf16[128,1024]{1,0:T(8,128)(2,1)S(1)} collective-permute-done((bf16[128,1024]{1,0:T(8,128)(2,1)}, bf16[128,1024]{1,0:T(8,128)(2,1)S(1)}, u32[]{:S(2)}, u32[]{:S(2)}) %collective-permute-start.20) | collective-permute-done | bytes 262176 | tf_op jit(solution)/shard_map/ppermute | solution.py:363
  127.7 0.1 collective-permute-start.26
  127.7 0.8 collective-permute-start.25
  128.6 1.9 %collective-permute-start.24 = (bf16[2,128,256]{2,1,0:T(8,128)(2,1)S(1)}, bf16[2,128,256]{2,1,0:T(8,128)(2,1)S(1)}, u32[]{:S(2)}, u32[]{:S(2)}) collective-permute-start(bf16[2,128,256]{2,1,0:T(8,128)(2,1)S(1)} %get-tuple-element.120), channel_id=1, source_target_pairs={{0,6},{2,0},{4,2},{6,4},{1,7},{3,1},{5,3},{7,5},{8,14},{10,8},{12,... | collective-permute-start | bytes 393224 | tf_op jit(solution)/shard_map/ppermute | solution.py:363
  130.5 0.1 convert_reduce_fusion
  130.5 0.7 collective-permute-start.27
  131.2 2.0 %shard_map.131 = (bf16[1,2,128,2048]{3,2,1,0:T(8,128)(2,1)}, bf16[1,2,128,2048]{3,2,1,0:T(8,128)(2,1)}) custom-call(s32[5]{0:T(128)S(1)} %stack.59.pos_ref, bf16[128,1024]{1,0:T(8,128)(2,1)S(1)} %get-tuple-element.94.refs_0_, bf16[128,1024]{1,0:T(8,128)(2,1)S(1)} %collective-permute-done.14.refs_1_, bf16[128,1024]{1,0:T(8,128)(2,1)S(1)} %collective-permute-done.15.refs_2_, ...), custom_call_target="tpu_custom_call" | custom-call | bytes 4194324 | tf_op jit(solution)/shard_map/pallas_call | solution.py:347
  133.2 3.2 %collective-permute-done.26.p3 = bf16[2,128,256]{2,1,0:T(8,128)(2,1)S(1)} collective-permute-done((bf16[2,128,256]{2,1,0:T(8,128)(2,1)S(1)}, bf16[2,128,256]{2,1,0:T(8,128)(2,1)S(1)}, u32[]{:S(2)}, u32[]{:S(2)}) %collective-permute-start.26) | collective-permute-done | bytes 131104 | tf_op jit(solution)/shard_map/ppermute | solution.py:363
  136.4 1.4 %shard_map.132 = (bf16[1,2,128,512]{3,2,1,0:T(8,128)(2,1)}, bf16[1,2,128,512]{3,2,1,0:T(8,128)(2,1)}) custom-call(s32[5]{0:T(128)S(1)} %stack.59.pos_ref, bf16[2,128,256]{2,1,0:T(8,128)(2,1)S(1)} %get-tuple-element.121.p0, bf16[2,128,256]{2,1,0:T(8,128)(2,1)S(1)} %collective-permute-done.24.p1, bf16[2,128,256]{2,1,0:T(8,128)(2,1)S(1)} %collective-permute-done.25.p2, ...), custom_call_target="tpu_custom_call" | custom-call | bytes 1048596 | tf_op jit(solution)/shard_map/pallas_call | solution.py:347
  137.8 0.6 slice_bitcast_fusion.10
  (50 shorter events, 0.2 us)
Async XLA Ops:
  1.4 0.7 collective-permute-start.3
  2.0 17.9 %collective-permute-start.6 = (bf16[32,256]{1,0:T(8,128)(2,1)S(1)}, bf16[32,256]{1,0:T(8,128)(2,1)S(1)}, u32[]{:S(2)}, u32[]{:S(2)}) collective-permute-start(bf16[32,256]{1,0:T(8,128)(2,1)S(1)} %collective-permute-done.3), channel_id=1, source_target_pairs={{0,96},{32,0},{64,32},{96,64},{1,97},{33,1},{65,33},{97,65},{2,98}... | collective-permute-start | bytes 49160 | tf_op jit(solution)/shard_map/ppermute | solution.py:384
  5.4 16.5 %collective-permute-start.5 = (bf16[32,256]{1,0:T(8,128)(2,1)S(1)}, bf16[32,256]{1,0:T(8,128)(2,1)S(1)}, u32[]{:S(2)}, u32[]{:S(2)}) collective-permute-start(bf16[32,256]{1,0:T(8,128)(2,1)S(1)} %collective-permute-done.3), channel_id=1, source_target_pairs={{0,64},{32,96},{64,0},{96,32},{1,65},{33,97},{65,1},{97,33},{2,66}... | collective-permute-start | bytes 49160 | tf_op jit(solution)/shard_map/ppermute | solution.py:384
  5.9 15.9 %collective-permute-start.4 = (bf16[32,256]{1,0:T(8,128)(2,1)S(1)}, bf16[32,256]{1,0:T(8,128)(2,1)S(1)}, u32[]{:S(2)}, u32[]{:S(2)}) collective-permute-start(bf16[32,256]{1,0:T(8,128)(2,1)S(1)} %collective-permute-done.3), channel_id=1, source_target_pairs={{0,32},{32,64},{64,96},{96,0},{1,33},{33,65},{65,97},{97,1},{2,34}... | collective-permute-start | bytes 49160 | tf_op jit(solution)/shard_map/ppermute | solution.py:384
  6.6 1.0 copy-start.2
  7.6 0.9 copy-start.3
  9.2 18.6 %collective-permute-start = (bf16[2,128,256]{2,1,0:T(8,128)(2,1)S(1)}, bf16[2,128,256]{2,1,0:T(8,128)(2,1)S(1)}, u32[]{:S(2)}, u32[]{:S(2)}) collective-permute-start(bf16[2,128,256]{2,1,0:T(8,128)(2,1)S(1)} %get-tuple-element.73), channel_id=1, source_target_pairs={{0,2},{2,4},{4,6},{6,0},{1,3},{3,5},{5,7},{7,1},{8,10},{10,12},{12... | collective-permute-start | bytes 393224 | tf_op jit(solution)/shard_map/ppermute | solution.py:363
  16.0 11.8 %collective-permute-start.1 = (bf16[2,128,256]{2,1,0:T(8,128)(2,1)S(1)}, bf16[2,128,256]{2,1,0:T(8,128)(2,1)S(1)}, u32[]{:S(2)}, u32[]{:S(2)}) collective-permute-start(bf16[2,128,256]{2,1,0:T(8,128)(2,1)S(1)} %get-tuple-element.74), channel_id=1, source_target_pairs={{0,4},{2,6},{4,0},{6,2},{1,5},{3,7},{5,1},{7,3},{8,12},{10,14},{12... | collective-permute-start | bytes 393224 | tf_op jit(solution)/shard_map/ppermute | solution.py:363
  19.9 8.0 %collective-permute-start.2 = (bf16[2,128,256]{2,1,0:T(8,128)(2,1)S(1)}, bf16[2,128,256]{2,1,0:T(8,128)(2,1)S(1)}, u32[]{:S(2)}, u32[]{:S(2)}) collective-permute-start(bf16[2,128,256]{2,1,0:T(8,128)(2,1)S(1)} %get-tuple-element.75), channel_id=1, source_target_pairs={{0,6},{2,0},{4,2},{6,4},{1,7},{3,1},{5,3},{7,5},{8,14},{10,8},{12,... | collective-permute-start | bytes 393224 | tf_op jit(solution)/shard_map/ppermute | solution.py:363
  21.9 5.9 %collective-permute-start.7 = (bf16[4,32,256]{2,1,0:T(8,128)(2,1)S(1)}, bf16[4,32,256]{2,1,0:T(8,128)(2,1)S(1)}, u32[]{:S(2)}, u32[]{:S(2)}) collective-permute-start(bf16[4,32,256]{2,1,0:T(8,128)(2,1)S(1)} %get-tuple-element.123), channel_id=1, source_target_pairs={{0,16},{16,0},{1,17},{17,1},{2,18},{18,2},{3,19},{19,3},{4,20},{20... | collective-permute-start | bytes 196616 | tf_op jit(solution)/shard_map/ppermute | solution.py:367
  23.6 1.2 copy-start
  24.8 1.2 copy-start.1
  27.7 0.7 copy-start.7
  27.7 0.8 copy-start.8
  27.7 0.9 copy-start.9
  28.6 18.7 %copy-start.12 = (s32[8,2]{0,1:T(2,128)S(1)}, s32[8,2]{0,1:T(2,128)}, u32[]{:S(2)}) copy-start(s32[8,2]{0,1:T(2,128)} %param.15) | copy-start | bytes 196
  28.6 13.9 %collective-permute-start.8 = (bf16[1280,256]{1,0:T(8,128)(2,1)S(1)}, bf16[1280,256]{1,0:T(8,128)(2,1)S(1)}, u32[]{:S(2)}, u32[]{:S(2)}) collective-permute-start(bf16[1280,256]{1,0:T(8,128)(2,1)S(1)} %fusion.6.rest_1_.rest_4_), channel_id=1, source_target_pairs={{0,8},{8,0},{1,9},{9,1},{2,10},{10,2},{3,11},{11,3},{4,12},{12,4},... | collective-permute-start | bytes 1966088 | tf_op jit(solution)/shard_map/ppermute | solution.py:367
  30.7 20.2 %all-to-all-start = ((bf16[4,128,1024]{2,1,0:T(8,128)(2,1)}), bf16[4,128,1024]{2,1,0:T(8,128)(2,1)S(1)}, u32[]{:S(2)}, u32[]{:S(2)}) async-start(bf16[4,128,1024]{2,1,0:T(8,128)(2,1)} %get-tuple-element.81), calls=%async_computation | async-start | bytes 2097152 | tf_op jit(solution)/shard_map/all_to_all | solution.py:359
  34.2 15.8 %collective-permute-start.12 = (bf16[1280,256]{1,0:T(8,128)(2,1)S(1)}, bf16[1280,256]{1,0:T(8,128)(2,1)S(1)}, u32[]{:S(2)}, u32[]{:S(2)}) collective-permute-start(bf16[1280,256]{1,0:T(8,128)(2,1)S(1)} %fusion.6.rest_1_.rest_4_), channel_id=1, source_target_pairs={{0,1},{1,0},{2,3},{3,2},{4,5},{5,4},{6,7},{7,6},{8,9},{9,8},{10,11... | collective-permute-start | bytes 1966088 | tf_op jit(solution)/shard_map/ppermute | solution.py:367
  42.5 8.3 %collective-permute-start.13 = (bf16[1280,256]{1,0:T(8,128)(2,1)S(1)}, bf16[1280,256]{1,0:T(8,128)(2,1)}, u32[]{:S(2)}, u32[]{:S(2)}) collective-permute-start(bf16[1280,256]{1,0:T(8,128)(2,1)S(1)} %collective-permute-done.8.rest_3_.rest_6_), channel_id=1, source_target_pairs={{0,1},{1,0},{2,3},{3,2},{4,5},{5,4},{6,7},{7,6},{8,9},{9,8},{10,11... | collective-permute-start | bytes 1966088 | tf_op jit(solution)/shard_map/ppermute | solution.py:367
  47.3 3.5 %copy-start.10 = (s32[8]{0:T(128)S(1)}, s32[8]{0:T(128)}, u32[]{:S(2)}) copy-start(s32[8]{0:T(128)} %cnt_ref.3) | copy-start | bytes 100
  47.3 23.9 %collective-permute-start.9 = (bf16[128,1024]{1,0:T(8,128)(2,1)}, bf16[128,1024]{1,0:T(8,128)(2,1)}, u32[]{:S(2)}, u32[]{:S(2)}) collective-permute-start(bf16[128,1024]{1,0:T(8,128)(2,1)} %copy-done.9), channel_id=1, source_target_pairs={{0,2},{2,4},{4,6},{6,0},{1,3},{3,5},{5,7},{7,1},{8,10},{10,12},{12... | collective-permute-start | bytes 786440 | tf_op jit(solution)/shard_map/ppermute | solution.py:363
  47.3 24.7 %collective-permute-start.10 = (bf16[128,1024]{1,0:T(8,128)(2,1)}, bf16[128,1024]{1,0:T(8,128)(2,1)}, u32[]{:S(2)}, u32[]{:S(2)}) collective-permute-start(bf16[128,1024]{1,0:T(8,128)(2,1)} %copy-done.8), channel_id=1, source_target_pairs={{0,4},{2,6},{4,0},{6,2},{1,5},{3,7},{5,1},{7,3},{8,12},{10,14},{12... | collective-permute-start | bytes 786440 | tf_op jit(solution)/shard_map/ppermute | solution.py:363
  48.5 32.8 %collective-permute-start.11 = (bf16[128,1024]{1,0:T(8,128)(2,1)}, bf16[128,1024]{1,0:T(8,128)(2,1)}, u32[]{:S(2)}, u32[]{:S(2)}) collective-permute-start(bf16[128,1024]{1,0:T(8,128)(2,1)} %copy-done.7), channel_id=1, source_target_pairs={{0,6},{2,0},{4,2},{6,4},{1,7},{3,1},{5,3},{7,5},{8,14},{10,8},{12,... | collective-permute-start | bytes 786440 | tf_op jit(solution)/shard_map/ppermute | solution.py:363
  50.0 0.8 copy-start.4
  50.9 1.1 copy-start.5
  52.0 29.4 %copy-start.6 = (bf16[1280,256]{1,0:T(8,128)(2,1)S(1)}, bf16[1280,256]{1,0:T(8,128)(2,1)}, u32[]{:S(2)}) copy-start(bf16[1280,256]{1,0:T(8,128)(2,1)} %copy-done.4) | copy-start | bytes 1966084
  68.7 30.5 %collective-permute-start.14 = (bf16[128,1024]{1,0:T(8,128)(2,1)S(1)}, bf16[128,1024]{1,0:T(8,128)(2,1)S(1)}, u32[]{:S(2)}, u32[]{:S(2)}) collective-permute-start(bf16[128,1024]{1,0:T(8,128)(2,1)S(1)} %get-tuple-element.90), channel_id=1, source_target_pairs={{0,6},{2,0},{4,2},{6,4},{1,7},{3,1},{5,3},{7,5},{8,14},{10,8},{12,... | collective-permute-start | bytes 786440 | tf_op jit(solution)/shard_map/ppermute | solution.py:363
  69.5 29.8 %collective-permute-start.15 = (bf16[128,1024]{1,0:T(8,128)(2,1)S(1)}, bf16[128,1024]{1,0:T(8,128)(2,1)S(1)}, u32[]{:S(2)}, u32[]{:S(2)}) collective-permute-start(bf16[128,1024]{1,0:T(8,128)(2,1)S(1)} %get-tuple-element.91), channel_id=1, source_target_pairs={{0,4},{2,6},{4,0},{6,2},{1,5},{3,7},{5,1},{7,3},{8,12},{10,14},{12... | collective-permute-start | bytes 786440 | tf_op jit(solution)/shard_map/ppermute | solution.py:363
  71.2 28.0 %collective-permute-start.16 = (bf16[128,1024]{1,0:T(8,128)(2,1)S(1)}, bf16[128,1024]{1,0:T(8,128)(2,1)S(1)}, u32[]{:S(2)}, u32[]{:S(2)}) collective-permute-start(bf16[128,1024]{1,0:T(8,128)(2,1)S(1)} %get-tuple-element.92), channel_id=1, source_target_pairs={{0,2},{2,4},{4,6},{6,0},{1,3},{3,5},{5,7},{7,1},{8,10},{10,12},{12... | collective-permute-start | bytes 786440 | tf_op jit(solution)/shard_map/ppermute | solution.py:363
  72.0 27.3 %collective-permute-start.17 = (bf16[2,4,128,256]{3,2,1,0:T(8,128)(2,1)S(1)}, bf16[2,4,128,256]{3,2,1,0:T(8,128)(2,1)S(1)}, u32[]{:S(2)}, u32[]{:S(2)}) collective-permute-start(bf16[2,4,128,256]{3,2,1,0:T(8,128)(2,1)S(1)} %get-tuple-element.93), channel_id=1, source_target_pairs={{0,8},{8,0},{1,9},{9,1},{2,10},{10,2},{3,11},{11,3},{4,12},{12,4},... | collective-permute-start | bytes 1572872 | tf_op jit(solution)/shard_map/ppermute | solution.py:367
  99.3 3.6 %collective-permute-start.22 = (bf16[2,4,128,256]{3,2,1,0:T(8,128)(2,1)S(1)}, bf16[2,4,128,256]{3,2,1,0:T(8,128)(2,1)S(1)}, u32[]{:S(2)}, u32[]{:S(2)}) collective-permute-start(bf16[2,4,128,256]{3,2,1,0:T(8,128)(2,1)S(1)} %get-tuple-element.105), channel_id=1, source_target_pairs={{0,1},{1,0},{2,3},{3,2},{4,5},{5,4},{6,7},{7,6},{8,9},{9,8},{10,11... | collective-permute-start | bytes 1572872 | tf_op jit(solution)/shard_map/ppermute | solution.py:367
  101.4 11.9 %collective-permute-start.21 = (bf16[4,128,256]{2,1,0:T(8,128)(2,1)S(1)}, bf16[4,128,256]{2,1,0:T(8,128)(2,1)S(1)}, u32[]{:S(2)}, u32[]{:S(2)}) collective-permute-start(bf16[4,128,256]{2,1,0:T(8,128)(2,1)S(1)} %fusion.2), channel_id=1, source_target_pairs={{0,1},{1,0},{2,3},{3,2},{4,5},{5,4},{6,7},{7,6},{8,9},{9,8},{10,11... | collective-permute-start | bytes 786440 | tf_op jit(solution)/shard_map/ppermute | solution.py:367
  102.9 10.5 %copy-start.11 = (bf16[2,4,128,256]{3,2,1,0:T(8,128)(2,1)}, bf16[2,4,128,256]{3,2,1,0:T(8,128)(2,1)S(1)}, u32[]{:S(2)}) copy-start(bf16[2,4,128,256]{3,2,1,0:T(8,128)(2,1)S(1)} %collective-permute-done.22) | copy-start | bytes 1572868
  103.7 15.0 %collective-permute-start.23 = (bf16[4,128,256]{2,1,0:T(8,128)(2,1)}, bf16[4,128,256]{2,1,0:T(8,128)(2,1)}, u32[]{:S(2)}, u32[]{:S(2)}) collective-permute-start(bf16[4,128,256]{2,1,0:T(8,128)(2,1)} %fusion.3), channel_id=1, source_target_pairs={{0,8},{8,0},{1,9},{9,1},{2,10},{10,2},{3,11},{11,3},{4,12},{12,4},... | collective-permute-start | bytes 786440 | tf_op jit(solution)/shard_map/ppermute | solution.py:367
  110.7 9.2 %collective-permute-start.18 = (bf16[128,1024]{1,0:T(8,128)(2,1)}, bf16[128,1024]{1,0:T(8,128)(2,1)S(1)}, u32[]{:S(2)}, u32[]{:S(2)}) collective-permute-start(bf16[128,1024]{1,0:T(8,128)(2,1)} %get-tuple-element.99), channel_id=1, source_target_pairs={{0,6},{2,0},{4,2},{6,4},{1,7},{3,1},{5,3},{7,5},{8,14},{10,8},{12,... | collective-permute-start | bytes 786440 | tf_op jit(solution)/shard_map/ppermute | solution.py:363
  112.7 8.7 %collective-permute-start.19 = (bf16[128,1024]{1,0:T(8,128)(2,1)}, bf16[128,1024]{1,0:T(8,128)(2,1)S(1)}, u32[]{:S(2)}, u32[]{:S(2)}) collective-permute-start(bf16[128,1024]{1,0:T(8,128)(2,1)} %get-tuple-element.100), channel_id=1, source_target_pairs={{0,4},{2,6},{4,0},{6,2},{1,5},{3,7},{5,1},{7,3},{8,12},{10,14},{12... | collective-permute-start | bytes 786440 | tf_op jit(solution)/shard_map/ppermute | solution.py:363
  112.7 14.9 %collective-permute-start.20 = (bf16[128,1024]{1,0:T(8,128)(2,1)}, bf16[128,1024]{1,0:T(8,128)(2,1)S(1)}, u32[]{:S(2)}, u32[]{:S(2)}) collective-permute-start(bf16[128,1024]{1,0:T(8,128)(2,1)} %get-tuple-element.101), channel_id=1, source_target_pairs={{0,2},{2,4},{4,6},{6,0},{1,3},{3,5},{5,7},{7,1},{8,10},{10,12},{12... | collective-permute-start | bytes 786440 | tf_op jit(solution)/shard_map/ppermute | solution.py:363
  113.4 17.0 %all-to-all-start.1 = ((bf16[32,2,32,128]{3,2,1,0:T(8,128)(2,1)}), bf16[32,2,32,128]{3,2,1,0:T(8,128)(2,1)S(1)}, u32[]{:S(2)}, u32[]{:S(2)}) async-start(bf16[32,2,32,128]{3,2,1,0:T(8,128)(2,1)} %bitcast.32), calls=%async_computation.1 | async-start | bytes 1048576 | tf_op jit(solution)/shard_map/all_to_all | solution.py:415
  127.7 8.7 %collective-permute-start.26 = (bf16[2,128,256]{2,1,0:T(8,128)(2,1)S(1)}, bf16[2,128,256]{2,1,0:T(8,128)(2,1)S(1)}, u32[]{:S(2)}, u32[]{:S(2)}) collective-permute-start(bf16[2,128,256]{2,1,0:T(8,128)(2,1)S(1)} %get-tuple-element.118), channel_id=1, source_target_pairs={{0,2},{2,4},{4,6},{6,0},{1,3},{3,5},{5,7},{7,1},{8,10},{10,12},{12... | collective-permute-start | bytes 393224 | tf_op jit(solution)/shard_map/ppermute | solution.py:363
  127.7 8.7 %collective-permute-start.25 = (bf16[2,128,256]{2,1,0:T(8,128)(2,1)S(1)}, bf16[2,128,256]{2,1,0:T(8,128)(2,1)S(1)}, u32[]{:S(2)}, u32[]{:S(2)}) collective-permute-start(bf16[2,128,256]{2,1,0:T(8,128)(2,1)S(1)} %get-tuple-element.119), channel_id=1, source_target_pairs={{0,4},{2,6},{4,0},{6,2},{1,5},{3,7},{5,1},{7,3},{8,12},{10,14},{12... | collective-permute-start | bytes 393224 | tf_op jit(solution)/shard_map/ppermute | solution.py:363
  128.6 7.8 %collective-permute-start.24 = (bf16[2,128,256]{2,1,0:T(8,128)(2,1)S(1)}, bf16[2,128,256]{2,1,0:T(8,128)(2,1)S(1)}, u32[]{:S(2)}, u32[]{:S(2)}) collective-permute-start(bf16[2,128,256]{2,1,0:T(8,128)(2,1)S(1)} %get-tuple-element.120), channel_id=1, source_target_pairs={{0,6},{2,0},{4,2},{6,4},{1,7},{3,1},{5,3},{7,5},{8,14},{10,8},{12,... | collective-permute-start | bytes 393224 | tf_op jit(solution)/shard_map/ppermute | solution.py:363
  130.5 7.3 %collective-permute-start.27 = (f32[2,32,128]{2,1,0:T(8,128)S(1)}, f32[2,32,128]{2,1,0:T(8,128)S(1)}, u32[]{:S(2)}, u32[]{:S(2)}) collective-permute-start(f32[2,32,128]{2,1,0:T(8,128)S(1)} %convert_reduce_fusion), channel_id=1, source_target_pairs={{0,0},{1,1},{8,2},{9,3},{2,4},{3,5},{10,6},{11,7},{4,8},{5,9},{12,... | collective-permute-start | bytes 98312 | tf_op jit(solution)/shard_map/ppermute | solution.py:424
